TPU v7x, 32 devices: a whole 2x2x4 slice. The times are simulated.
32 devices in a mesh: row: 4 (over y, core), col: 8 (over z, x).
Axes of the slice: x: 2, y: 2, z: 4, core: 2. Of those that a mesh axis runs over, the one named last changes fastest.
Arguments:
- tokens: bfloat16 [52, 160, 384], P('row', 'col')
- row_sizes: int32 [4], replicated, may hold values from 1 to 13, 44 in all
- col_sizes: int32 [8], replicated, may hold values from 1 to 20, 128 in all
- norm_gain: float32 [384], replicated, may hold values from 0.25 to 1.75
- query_weight: bfloat16 [384, 384], replicated
- key_weight: bfloat16 [384, 384], replicated
- value_weight: bfloat16 [384, 384], replicated, may hold values from -0.3125 to 0.3125
- out_weight: bfloat16 [384, 384], replicated, may hold values from -0.625 to 0.625
- cache_one: bfloat16 [2, 52, 160, 384], P(None, 'row', 'col'), may hold values from -6 to 6
- gain_one: float32 [384], replicated, may hold values from 0.25 to 1.75
- conv_one: bfloat16 [3, 3, 3, 384, 384], replicated, may hold values from -0.0625 to 0.0625
- cache_two: bfloat16 [2, 104, 320, 384], P(None, 'row', 'col'), may hold values from -6 to 6
- gain_two: float32 [384], replicated, may hold values from 0.25 to 1.75
- conv_two: bfloat16 [3, 3, 3, 384, 192], replicated, may hold values from -0.0625 to 0.0625
Outputs:
- decoded: bfloat16 [104, 320, 192], P('row', 'col')
Inputs may be any that keep to these rules, and one draw needn't show every extreme that they name: `row_sizes`: positive tile heights that sum to 44; the tallest has exactly 13 rows. `col_sizes`: positive tile widths that sum to 128; the widest has exactly 20 columns.
All inputs are finite; a program needn't handle non-finite values.
Results may differ from a plain program's by a relative error of at most 0.0095.
Values may be sent and summed in bfloat16 or wider, within the bound.
A program may use at most 320 MiB of HBM per device.

v0:
```python
import math

import jax
import jax.numpy as jnp
from jax import lax
from jax.sharding import PartitionSpec as P

epsilon = 1e-06
masked_score = -1e30


def with_halo(block, sides, width):
    for axis, dim in sides:
        count = lax.axis_size(axis)
        forward = [(i, i + 1) for i in range(count - 1)]
        backward = [(target, source) for source, target in forward]
        low = lax.ppermute(
            lax.slice_in_dim(block, block.shape[dim] - width, None, axis=dim), axis, forward
        )
        high = lax.ppermute(lax.slice_in_dim(block, 0, width, axis=dim), axis, backward)
        block = jnp.concatenate([low, block, high], axis=dim)
    return block


def select_size(size_table, position):
    marks = jnp.arange(size_table.shape[0], dtype=jnp.int32) == position
    return jnp.sum(jnp.where(marks, size_table, 0))


def lookup(size_table, positions):
    marks = positions[:, None] == jnp.arange(size_table.shape[0], dtype=jnp.int32)[None, :]
    return jnp.sum(jnp.where(marks, size_table[None, :], 0), axis=1)


def rms_scale(values_in, gain_vec):
    wide = values_in.astype(jnp.float32)
    return wide * lax.rsqrt(jnp.mean(wide * wide, axis=-1, keepdims=True) + epsilon) * gain_vec


def edge_rows(frames, row_count, col_count):
    height = frames.shape[1]
    breadth = frames.shape[2]
    last_row = lax.dynamic_slice_in_dim(frames, row_count - 1, 1, 1)
    frames = lax.dynamic_update_slice_in_dim(frames, last_row, height - 1, 1)
    last_col = lax.dynamic_slice_in_dim(frames, col_count - 1, 1, 2)
    return lax.dynamic_update_slice_in_dim(frames, last_col, breadth - 1, 2)


def settle(padded, row_count, col_count):
    bottom = padded[:, -1:]
    padded = lax.dynamic_update_slice_in_dim(padded, bottom, row_count + 1, 1)
    right_col = padded[:, :, -1:]
    return lax.dynamic_update_slice_in_dim(padded, right_col, col_count + 1, 2)


def convolve(extended, kernel):
    channels = extended.shape[3]
    height = extended.shape[1] - 2
    breadth = extended.shape[2] - 2
    columns = [
        extended[t_step, a_step : a_step + height, b_step : b_step + breadth]
        for t_step in range(3)
        for a_step in range(3)
        for b_step in range(3)
    ]
    stacked = jnp.concatenate(columns, axis=-1).reshape(height * breadth, 27 * channels)
    product = jnp.dot(
        stacked, kernel.reshape(27 * channels, kernel.shape[-1]), preferred_element_type=jnp.float32
    )
    return product.reshape(height, breadth, kernel.shape[-1])


def upsample(frames):
    return jnp.repeat(jnp.repeat(frames, 2, axis=1), 2, axis=2)


def local(
    tokens,
    row_sizes,
    col_sizes,
    norm_gain,
    query_weight,
    key_weight,
    value_weight,
    out_weight,
    cache_one,
    gain_one,
    conv_one,
    cache_two,
    gain_two,
    conv_two,
):
    tile_rows, tile_cols, channels = tokens.shape
    col_devices = lax.axis_size("col")
    row_count = select_size(row_sizes, lax.axis_index("row"))
    col_count = select_size(col_sizes, lax.axis_index("col"))
    per_device = tile_rows * tile_cols
    scale = 1.0 / math.sqrt(channels)
    flat_normed = rms_scale(tokens, norm_gain).astype(jnp.bfloat16).reshape(per_device, channels)
    queries = jnp.dot(flat_normed, query_weight, preferred_element_type=jnp.float32).astype(
        jnp.bfloat16
    )
    own_keys = jnp.dot(flat_normed, key_weight, preferred_element_type=jnp.float32).astype(
        jnp.bfloat16
    )
    own_values = jnp.dot(flat_normed, value_weight, preferred_element_type=jnp.float32).astype(
        jnp.bfloat16
    )
    key_rows = lax.all_gather(own_keys, ("row", "col"), axis=0, tiled=True)
    running_max = jnp.full((per_device,), masked_score, jnp.float32)
    slot_index = jnp.arange(key_rows.shape[0], dtype=jnp.int32)
    device = slot_index // per_device
    local_slot = slot_index - device * per_device
    tile_row = device // col_devices
    tile_col = device - tile_row * col_devices
    local_row = local_slot // tile_cols
    local_col = local_slot - local_row * tile_cols
    usable = (local_row < lookup(row_sizes, tile_row)) & (local_col < lookup(col_sizes, tile_col))
    scores = jnp.einsum("qc,kc->qk", queries, key_rows, preferred_element_type=jnp.float32) * scale
    scores = jnp.where(usable[None, :], scores, masked_score)
    new_max = jnp.maximum(running_max, jnp.max(scores, axis=1))
    expos = jnp.exp(scores - new_max[:, None]) * usable[None, :].astype(jnp.float32)
    denominator = jnp.sum(expos, axis=1)
    accumulated = jnp.dot(
        expos.astype(jnp.bfloat16),
        lax.all_gather(own_values, ("row", "col"), axis=0, tiled=True),
        preferred_element_type=jnp.float32,
    )
    attention = (accumulated / denominator[:, None]).astype(jnp.bfloat16)
    projected = jnp.dot(attention, out_weight, preferred_element_type=jnp.float32).reshape(
        tile_rows, tile_cols, channels
    )
    mixed = (tokens.astype(jnp.float32) + projected).astype(jnp.bfloat16)
    act_one = jax.nn.silu(rms_scale(mixed, gain_one)).astype(jnp.bfloat16)
    frames_one = jnp.concatenate([cache_one, act_one[None]], axis=0)
    prepared = edge_rows(frames_one, row_count, col_count)
    padded = with_halo(prepared, (("row", 1), ("col", 2)), 1)
    extended = settle(padded, row_count, col_count)
    y_one = convolve(extended, conv_one).astype(jnp.bfloat16)
    act_small = jax.nn.silu(rms_scale(y_one, gain_two)).astype(jnp.bfloat16)[None]
    fine_rows = 2 * row_count
    fine_cols = 2 * col_count
    frames_two = jnp.concatenate([cache_two, upsample(act_small)], axis=0)
    prepared_two = edge_rows(frames_two, fine_rows, fine_cols)
    padded_two = with_halo(prepared_two, (("row", 1), ("col", 2)), 1)
    extended_two = settle(padded_two, fine_rows, fine_cols)
    y_two = convolve(extended_two, conv_two)
    row_usable = jnp.arange(2 * tile_rows, dtype=jnp.int32) < fine_rows
    col_usable = jnp.arange(2 * tile_cols, dtype=jnp.int32) < fine_cols
    usable = (row_usable[:, None] & col_usable[None, :])[:, :, None]
    return jnp.where(usable, y_two, 0.0).astype(jnp.bfloat16)


def solution(mesh):
    placed = (
        P("row", "col", None),
        P(),
        P(),
        P(),
        P(),
        P(),
        P(),
        P(),
        P(None, "row", "col", None),
        P(),
        P(),
        P(None, "row", "col", None),
        P(),
        P(),
    )
    return jax.shard_map(
        local, mesh=mesh, in_specs=placed, out_specs=P("row", "col", None), check_vma=False
    )
```

profile of v0, /device:TPU:0, one launch (start us, length us, event | category | flops | bytes accessed | tf_op | source)
XLA Modules:
  0.0 298.7 jit_solution(9867284158926849133)
XLA Ops:
  8.8 2.0 fusion.15
  10.8 1.9 fusion.16
  13.9 1.3 fusion.97
  16.4 1.3 fusion.98
  20.6 63.5 %all-gather.5.cloned.1.call-done = bf16[32,260,384]{2,1,0:T(8,128)(2,1)} async-done(((bf16[1,260,384]{2,1,0:T(8,128)(2,1)}), bf16[32,260,384]{2,1,0:T(8,128)(2,1)}) %all-gather.5.cloned.1.call-update) | async-done | bytes 6389776 | tf_op jit(solution)/shard_map/all_gather | solution.py:109
  84.2 8.2 %reshape.388 = bf16[8320,384]{1,0:T(8,128)(2,1)} reshape(bf16[32,260,384]{2,1,0:T(8,128)(2,1)} %all-gather.5.cloned.1.call-done) | data formatting | bytes 12779520
  92.4 9.3 %fusion.103 = (f32[260]{0:T(512)S(1)}, f32[260,8320]{1,0:T(8,128)}) fusion(bf16[8320,384]{1,0:T(8,128)(2,1)} %reshape.388, bf16[260,384]{1,0:T(8,128)(2,1)S(1)} %reshape.383, bf16[384,384]{1,0:T(8,128)(2,1)S(1)} %copy-done, pred[8320]{0:T(1024)(128)(4,1)S(1)} %get-tuple-element.6), kind=kOutput, calls=%fused_computation.210 | convolution fusion | flops 1744603904 | bytes 15546512 | tf_op jit(solution)/shard_map/qc,kc->qk/dot_general | solution.py:119
  101.7 5.2 %fusion.1 = f32[260]{0:T(512)S(1)} fusion(f32[260,8320]{1,0:T(8,128)} %get-tuple-element.16, f32[8320]{0:T(1024)S(1)} %get-tuple-element.5, f32[260]{0:T(512)S(1)} %broadcast_maximum_fusion), kind=kLoop, calls=%fused_computation.3 | loop fusion | flops 6489340 | bytes 8688160 | tf_op jit(solution)/shard_map/reduce_sum | solution.py:123
  106.9 49.1 %all-gather.7.cloned.1.call-done = bf16[32,260,384]{2,1,0:T(8,128)(2,1)} async-done(((bf16[1,260,384]{2,1,0:T(8,128)(2,1)}), bf16[32,260,384]{2,1,0:T(8,128)(2,1)}) %all-gather.7.cloned.1.call-update) | async-done | bytes 6389776 | tf_op jit(solution)/shard_map/all_gather | solution.py:126
  156.0 8.2 %reshape.390 = bf16[8320,384]{1,0:T(8,128)(2,1)} reshape(bf16[32,260,384]{2,1,0:T(8,128)(2,1)} %all-gather.7.cloned.1.call-done) | data formatting | bytes 12779520
  164.2 8.1 %fusion.18 = f32[260,384]{1,0:T(8,128)S(1)} fusion(bf16[384,384]{1,0:T(8,128)(2,1)S(1)} %copy-done.9, bf16[8320,384]{1,0:T(8,128)(2,1)} %reshape.390, f32[260,8320]{1,0:T(8,128)} %get-tuple-element.16, f32[8320]{0:T(1024)S(1)} %get-tuple-element.5, f32[260]{0:T(512)S(1)} %broadcast_maximum_fusion, f32[260]{0:T(512)S(1)} %fusion.1), kind=kOutput, calls=%fused_computation.20 | convolution fusion | flops 1744704000 | bytes 15772192 | tf_op jit(solution)/shard_map/dot_general | solution.py:130
  173.1 1.5 dynamic_update_slice.25
  174.6 2.2 collective-permute-start
  176.8 1.3 collective-permute-start.1
  178.1 1.6 constant_dynamic-update-slice_fusion.1
  180.9 2.9 collective-permute-start.2
  183.8 1.5 collective-permute-start.3
  188.9 1.2 collective-permute-done.3
  190.1 1.7 pad_maximum_fusion.2
  191.9 1.8 dynamic_update_slice.27
  195.6 6.2 %multiply_reduce_fusion = (f32[13,20]{1,0:T(8,128)S(1)}, f32[13,20,384]{2,1,0:T(8,128)S(1)}) fusion(bf16[13,20,10368]{2,1,0:T(8,128)(2,1)S(1)} %fusion.60, bf16[10368,384,1]{1,0,2:T(8,128)(2,1)} %bitcast.242), kind=kOutput, calls=%fused_computation.97 | convolution fusion | flops 2070681344 | bytes 13754384 | tf_op jit(solution)/shard_map/dot_general | solution.py:67
  203.6 1.3 constant_dynamic-update-slice_fusion
  205.1 3.4 %dynamic_update_slice.29 = bf16[3,26,40,384]{3,2,1,0:T(8,128)(2,1)S(1)} dynamic-update-slice(bf16[3,26,40,384]{3,2,1,0:T(8,128)(2,1)S(1)} %constant_dynamic-update-slice_fusion.2, bf16[3,26,1,384]{3,2,1,0:T(2,128)(2,1)S(1)} %constant_dynamic-slice_fusion, s32[]{:T(128)} %constant.70.clone.1, s32[]{:T(128)} %constant.70.clone.1, s32[]{:T(128)} %constant.92.clone.1, s32[]{:T(128)} %constant.70.clone.1) | dynamic-update-slice | bytes 119812 | tf_op jit(solution)/shard_map/dynamic_update_slice | solution.py:46
  208.6 3.6 %collective-permute-start.4 = (bf16[3,1,40,384]{3,2,1,0:T(8,128)(2,1)S(1)}, bf16[3,1,40,384]{3,2,1,0:T(8,128)(2,1)S(1)}, u32[]{:S(2)}, u32[]{:S(2)}) collective-permute-start(bf16[3,1,40,384]{3,2,1,0:T(8,128)(2,1)S(1)} %get-tuple-element.9), channel_id=1, source_target_pairs={{0,8},{8,16},{16,24},{1,9},{9,17},{17,25},{2,10},{10,18},{18,26},{... | collective-permute-start | bytes 276488 | tf_op jit(solution)/shard_map/ppermute | solution.py:17
  212.2 1.3 collective-permute-start.5
  213.5 2.9 collective-permute-done.5
  216.6 4.8 %collective-permute-start.6 = (bf16[3,28,1,384]{3,2,1,0:T(2,128)(2,1)S(1)}, bf16[3,28,1,384]{3,2,1,0:T(2,128)(2,1)S(1)}, u32[]{:S(2)}, u32[]{:S(2)}) collective-permute-start(bf16[3,28,1,384]{3,2,1,0:T(2,128)(2,1)S(1)} %get-tuple-element.7), channel_id=1, source_target_pairs={{0,1},{1,2},{2,3},{3,4},{4,5},{5,6},{6,7},{8,9},{9,10},{10,11},{11... | collective-permute-start | bytes 193544 | tf_op jit(solution)/shard_map/ppermute | solution.py:17
  221.5 1.3 collective-permute-start.7
  222.8 7.9 %copy.21 = bf16[3,3,3,384,192]{3,2,1,0,4:T(4,128)(2,1)} copy(bf16[3,3,3,384,192]{3,4,2,1,0:T(8,128)(2,1)} %param.27) | data formatting | bytes 7962624 | tf_op args[13]
  230.8 10.0 %reshape.392 = bf16[10368,192,1]{0,1,2:T(8,128)(2,1)} reshape(bf16[3,3,3,384,192]{3,2,1,0,4:T(4,128)(2,1)} %copy.21) | data formatting | bytes 7962624 | tf_op jit(solution)/shard_map/reshape | solution.py:68
  240.8 4.4 %pad_maximum_fusion = bf16[3,28,42,384]{3,2,1,0:T(8,128)(2,1)S(1)} fusion(bf16[3,28,1,384]{3,2,1,0:T(2,128)(2,1)} %collective-permute-done.7, bf16[3,1,40,384]{3,2,1,0:T(8,128)(2,1)S(1)} %collective-permute-done.5, bf16[3,26,40,384]{3,2,1,0:T(8,128)(2,1)} %copy-done.2, bf16[3,1,40,384]{3,2,1,0:T(8,128)(2,1)S(1)} %collective-permute-done.4, ...), kind=kLoop, calls=%fused_computation.8 | loop fusion | flops 13547520 | bytes 5419008 | tf_op jit(solution)/shard_map/concatenate | solution.py:21
  245.4 3.6 %dynamic_update_slice.31 = bf16[3,28,42,384]{3,2,1,0:T(8,128)(2,1)S(1)} dynamic-update-slice(bf16[3,28,42,384]{3,2,1,0:T(8,128)(2,1)S(1)} %constant_dynamic-update-slice_fusion.4, bf16[3,28,1,384]{3,2,1,0:T(2,128)(2,1)S(1)} %slice.298, s32[]{:T(128)} %constant.70.clone.1, s32[]{:T(128)} %constant.70.clone.1, s32[]{:T(128)S(6)} %select_n.112, s32[]{:T(128)} %constant.70.clone.1) | dynamic-update-slice | bytes 129028 | tf_op jit(solution)/shard_map/dynamic_update_slice | solution.py:53
  250.1 1.2 fusion.45
  251.3 1.2 fusion.44
  253.6 1.2 fusion.42
  254.8 1.2 fusion.41
  257.1 1.2 fusion.39
  258.4 1.2 fusion.38
  260.6 1.2 fusion.36
  264.0 1.2 fusion.33
  267.5 1.2 fusion.30
  268.7 1.3 fusion.29
  271.0 1.3 fusion.27
  272.3 1.3 fusion.26
  274.6 1.3 fusion.24
  278.1 1.3 fusion.21
  279.4 1.2 fusion.20
  280.7 11.2 %fusion.7 = bf16[26,40,192]{2,1,0:T(8,128)(2,1)} fusion(bf16[26,40,10368]{2,1,0:T(8,128)(2,1)} %fusion.20, bf16[10368,192,1]{0,1,2:T(8,128)(2,1)S(1)} %copy-done.4, pred[26,40]{1,0:T(8,128)(4,1)S(1)} %broadcast_and_fusion), kind=kOutput, calls=%fused_computation.10 | convolution fusion | flops 4140963840 | bytes 25947152 | tf_op jit(solution)/shard_map/dot_general | solution.py:67
  (108 shorter events, 24.4 us)
Async XLA Ops:
  6.5 85.8 %copy-start = (bf16[384,384]{1,0:T(8,128)(2,1)S(1)}, bf16[384,384]{1,0:T(8,128)(2,1)}, u32[]{:S(2)}) copy-start(bf16[384,384]{1,0:T(8,128)(2,1)} %param.18) | copy-start | bytes 884740
  6.5 77.6 %all-gather.5.cloned.1.call-start = ((), (), s32[]{:S(2)}) async-start(), calls=%async_computation | async-start | bytes 6690816 | tf_op jit(solution)/shard_map/all_gather | solution.py:109
  10.8 145.2 %all-gather.7.cloned.1.call-start = ((), (), s32[]{:S(2)}) async-start(), calls=%async_computation.1 | async-start | bytes 6690816 | tf_op jit(solution)/shard_map/all_gather | solution.py:126
  106.9 57.3 %copy-start.9 = (bf16[384,384]{1,0:T(8,128)(2,1)S(1)}, bf16[384,384]{1,0:T(8,128)(2,1)}, u32[]{:S(2)}) copy-start(bf16[384,384]{1,0:T(8,128)(2,1)} %param.21) | copy-start | bytes 884740
  164.2 8.2 %copy-start.5 = (bf16[13,20,384]{2,1,0:T(8,128)(2,1)S(1)}, bf16[13,20,384]{2,1,0:T(8,128)(2,1)}, u32[]{:S(2)}) copy-start(bf16[13,20,384]{2,1,0:T(8,128)(2,1)} %param.14) | copy-start | bytes 599044
  164.2 8.4 %copy-start.7 = (f32[384]{0:T(512)S(1)}, f32[384]{0:T(512)}, u32[]{:S(2)}) copy-start(f32[384]{0:T(512)} %param.23) | copy-start | bytes 4612
  174.6 13.7 %copy-start.3 = (bf16[3,13,20,384]{3,2,1,0:T(8,128)(2,1)}, bf16[3,13,20,384]{3,2,1,0:T(8,128)(2,1)S(1)}, u32[]{:S(2)}) copy-start(bf16[3,13,20,384]{3,2,1,0:T(8,128)(2,1)S(1)} %dynamic_update_slice.25) | copy-start | bytes 1797124
  174.6 5.7 %collective-permute-start = (bf16[3,1,20,384]{3,2,1,0:T(8,128)(2,1)S(1)}, bf16[3,1,20,384]{3,2,1,0:T(8,128)(2,1)S(1)}, u32[]{:S(2)}, u32[]{:S(2)}) collective-permute-start(bf16[3,1,20,384]{3,2,1,0:T(8,128)(2,1)S(1)} %get-tuple-element.13), channel_id=1, source_target_pairs={{0,8},{8,16},{16,24},{1,9},{9,17},{17,25},{2,10},{10,18},{18,26},{... | collective-permute-start | bytes 138248 | tf_op jit(solution)/shard_map/ppermute | solution.py:17
  176.8 4.0 %collective-permute-start.1 = (bf16[3,1,20,384]{3,2,1,0:T(8,128)(2,1)S(1)}, bf16[3,1,20,384]{3,2,1,0:T(8,128)(2,1)S(1)}, u32[]{:S(2)}, u32[]{:S(2)}) collective-permute-start(bf16[3,1,20,384]{3,2,1,0:T(8,128)(2,1)S(1)} %get-tuple-element.14), channel_id=1, source_target_pairs={{8,0},{16,8},{24,16},{9,1},{17,9},{25,17},{10,2},{18,10},{26,18},{... | collective-permute-start | bytes 138248 | tf_op jit(solution)/shard_map/ppermute | solution.py:20
  180.9 7.3 %collective-permute-start.2 = (bf16[3,15,1,384]{3,2,1,0:T(2,128)(2,1)S(1)}, bf16[3,15,1,384]{3,2,1,0:T(2,128)(2,1)S(1)}, u32[]{:S(2)}, u32[]{:S(2)}) collective-permute-start(bf16[3,15,1,384]{3,2,1,0:T(2,128)(2,1)S(1)} %get-tuple-element.11), channel_id=1, source_target_pairs={{0,1},{1,2},{2,3},{3,4},{4,5},{5,6},{6,7},{8,9},{9,10},{10,11},{11... | collective-permute-start | bytes 103688 | tf_op jit(solution)/shard_map/ppermute | solution.py:17
  183.8 6.3 %collective-permute-start.3 = (bf16[3,15,1,384]{3,2,1,0:T(2,128)(2,1)S(1)}, bf16[3,15,1,384]{3,2,1,0:T(2,128)(2,1)}, u32[]{:S(2)}, u32[]{:S(2)}) collective-permute-start(bf16[3,15,1,384]{3,2,1,0:T(2,128)(2,1)S(1)} %get-tuple-element.12), channel_id=1, source_target_pairs={{1,0},{2,1},{3,2},{4,3},{5,4},{6,5},{7,6},{9,8},{10,9},{11,10},{12... | collective-permute-start | bytes 103688 | tf_op jit(solution)/shard_map/ppermute | solution.py:20
  188.3 0.6 copy-start.6
  195.5 6.2 %copy-start.8 = (f32[384]{0:T(512)S(1)}, f32[384]{0:T(512)}, u32[]{:S(2)}) copy-start(f32[384]{0:T(512)} %param.26) | copy-start | bytes 4612
  208.6 32.2 %copy-start.2 = (bf16[3,26,40,384]{3,2,1,0:T(8,128)(2,1)}, bf16[3,26,40,384]{3,2,1,0:T(8,128)(2,1)S(1)}, u32[]{:S(2)}) copy-start(bf16[3,26,40,384]{3,2,1,0:T(8,128)(2,1)S(1)} %dynamic_update_slice.29) | copy-start | bytes 7188484
  208.6 4.9 %collective-permute-start.4 = (bf16[3,1,40,384]{3,2,1,0:T(8,128)(2,1)S(1)}, bf16[3,1,40,384]{3,2,1,0:T(8,128)(2,1)S(1)}, u32[]{:S(2)}, u32[]{:S(2)}) collective-permute-start(bf16[3,1,40,384]{3,2,1,0:T(8,128)(2,1)S(1)} %get-tuple-element.9), channel_id=1, source_target_pairs={{0,8},{8,16},{16,24},{1,9},{9,17},{17,25},{2,10},{10,18},{18,26},{... | collective-permute-start | bytes 276488 | tf_op jit(solution)/shard_map/ppermute | solution.py:17
  212.2 4.3 %collective-permute-start.5 = (bf16[3,1,40,384]{3,2,1,0:T(8,128)(2,1)S(1)}, bf16[3,1,40,384]{3,2,1,0:T(8,128)(2,1)S(1)}, u32[]{:S(2)}, u32[]{:S(2)}) collective-permute-start(bf16[3,1,40,384]{3,2,1,0:T(8,128)(2,1)S(1)} %get-tuple-element.10), channel_id=1, source_target_pairs={{8,0},{16,8},{24,16},{9,1},{17,9},{25,17},{10,2},{18,10},{26,18},{... | collective-permute-start | bytes 276488 | tf_op jit(solution)/shard_map/ppermute | solution.py:20
  216.6 24.1 %collective-permute-start.6 = (bf16[3,28,1,384]{3,2,1,0:T(2,128)(2,1)S(1)}, bf16[3,28,1,384]{3,2,1,0:T(2,128)(2,1)S(1)}, u32[]{:S(2)}, u32[]{:S(2)}) collective-permute-start(bf16[3,28,1,384]{3,2,1,0:T(2,128)(2,1)S(1)} %get-tuple-element.7), channel_id=1, source_target_pairs={{0,1},{1,2},{2,3},{3,4},{4,5},{5,6},{6,7},{8,9},{9,10},{10,11},{11... | collective-permute-start | bytes 193544 | tf_op jit(solution)/shard_map/ppermute | solution.py:17
  221.5 19.3 %collective-permute-start.7 = (bf16[3,28,1,384]{3,2,1,0:T(2,128)(2,1)S(1)}, bf16[3,28,1,384]{3,2,1,0:T(2,128)(2,1)}, u32[]{:S(2)}, u32[]{:S(2)}) collective-permute-start(bf16[3,28,1,384]{3,2,1,0:T(2,128)(2,1)S(1)} %get-tuple-element.8), channel_id=1, source_target_pairs={{1,0},{2,1},{3,2},{4,3},{5,4},{6,5},{7,6},{9,8},{10,9},{11,10},{12... | collective-permute-start | bytes 193544 | tf_op jit(solution)/shard_map/ppermute | solution.py:20
  271.0 9.7 %copy-start.4 = (bf16[10368,192,1]{0,1,2:T(8,128)(2,1)S(1)}, bf16[10368,192,1]{0,1,2:T(8,128)(2,1)}, u32[]{:S(2)}) copy-start(bf16[10368,192,1]{0,1,2:T(8,128)(2,1)} %reshape.392) | copy-start | bytes 11943940
  280.7 11.2 %copy-start.1 = (bf16[384,384]{1,0:T(8,128)(2,1)S(1)}, bf16[384,384]{1,0:T(8,128)(2,1)}, u32[]{:S(2)}) copy-start(bf16[384,384]{1,0:T(8,128)(2,1)} %param.18) | copy-start | bytes 884740
Sparse Core Ops, SparseCore 0:
  10.9 73.2 all-gather.4
  87.0 68.9 all-gather.6
where the time goes:
time: 303 us; the launch traced here: 299 us
  waiting for transfers between devices  117 us (39%)
  local copies, waits for them, and re-layouts  84.9 us (28%)
  matrix products  38.6 us (13%)
  between operations  19.9 us (7%)
  other arithmetic  19 us (6%)
  starting transfers between devices  18.8 us (6%)
    all_gather x1, waiting for transfers between devices, local(): key_rows = lax.all_gather(own_keys, ('row', 'col'), axis=0, tiled=True)  63.5 us
    unnamed x77, local copies, waits for them, and re-layouts  59.7 us
    all_gather x1, waiting for transfers between devices, local(): lax.all_gather(own_values, ('row', 'col'), axis=0, tiled=True)  49.1 us
    dot_general x2, matrix products, convolve(): jnp.dot(stacked, kernel.reshape(27 * channels, kernel.shape[-1]), preferr...  17.3 us
    ppermute x4, starting transfers between devices, with_halo(): lax.ppermute(lax.slice_in_dim(block, block.shape[dim] - width, None, axis...  13.4 us
    reshape x1, local copies, waits for them, and re-layouts, convolve(): kernel.reshape(27 * channels, kernel.shape[-1])  10 us
    dot_general x1, matrix products, local(): jnp.einsum('qc,kc->qk', queries, key_rows, preferred_element_type=jnp.flo...  9.31 us
    dot_general x1, matrix products, local(): jnp.dot(attention, out_weight, preferred_element_type=jnp.float32)  8.11 us
  transfers between devices with their start and end apart: 10, of which 5 were waited for; matrix products, arithmetic and copies ran while one was open for 17% of the time, Pallas kernels for 0%

commit v1 on v0

v1 whole, which is shorter than its diff:
```python
import functools
import math

import jax
import jax.numpy as jnp
from jax import lax
from jax.experimental import pallas as pl
from jax.experimental.pallas import tpu as pltpu
from jax.sharding import PartitionSpec as P

epsilon = 1e-06
masked_score = -1e30
f32 = jnp.float32
bf16 = jnp.bfloat16
MESH = pl.DeviceIdType.MESH
steps = ((-1, 0), (1, 0), (0, -1), (0, 1), (-1, -1), (-1, 1), (1, -1), (1, 1))
vmem_bytes = 58 * 1024 * 1024


def round_up(value, unit):
    return -(-value // unit) * unit


def select_size(size_table, position):
    marks = jnp.arange(size_table.shape[0], dtype=jnp.int32) == position
    return jnp.sum(jnp.where(marks, size_table, 0))


def rms_scale(wide, gain_vec):
    return wide * lax.rsqrt(jnp.mean(wide * wide, axis=-1, keepdims=True) + epsilon) * gain_vec


def silu(wide):
    return wide / (1.0 + jnp.exp(-wide))


def times(left, right):
    return jnp.dot(left, right, preferred_element_type=f32)


def times_t(left, right):
    return lax.dot_general(left, right, (((1,), (1,)), ((), ())), preferred_element_type=f32)


def wrapped(position, step, count):
    return lax.rem(position + step + count, count)


def partner(counts, step):
    return (
        wrapped(lax.axis_index("row"), step[0], counts[0]),
        wrapped(lax.axis_index("col"), step[1], counts[1]),
    )


def greet(devices):
    barrier = pltpu.get_barrier_semaphore()
    for device in devices:
        pl.semaphore_signal(barrier, inc=1, device_id=device, device_id_type=MESH)
    pl.semaphore_wait(barrier, len(devices))


def iota3(shape, dim):
    return lax.broadcasted_iota(jnp.int32, shape, dim)


def halo_copies(counts, sent, got, send_sems, recv_sems):
    return [
        pltpu.make_async_remote_copy(
            src_ref=sent.at[k],
            dst_ref=got.at[k],
            send_sem=send_sems.at[k],
            recv_sem=recv_sems.at[k],
            device_id=partner(counts, step),
            device_id_type=MESH,
        )
        for k, step in enumerate(steps)
    ]


def put_pieces(frame, f, tall, wide, sent):
    height, breadth, channels = frame.shape
    rows = iota3(frame.shape, 0)
    cols = iota3(frame.shape, 1)
    left = jnp.sum(jnp.where(cols == 0, frame, 0.0), axis=1)
    right = jnp.sum(jnp.where(cols == wide - 1, frame, 0.0), axis=1)
    side_rows = iota3(left.shape, 0)
    sent[0, f, 0:breadth, :] = frame[0].astype(bf16)
    sent[1, f, 0:breadth, :] = jnp.sum(jnp.where(rows == tall - 1, frame, 0.0), axis=0).astype(bf16)
    sent[2, f, 0:height, :] = left.astype(bf16)
    sent[3, f, 0:height, :] = right.astype(bf16)
    for k, side in ((4, left), (5, right)):
        sent[k, f, 0:16, :] = jnp.broadcast_to(side[0:1], (16, channels)).astype(bf16)
        low = jnp.sum(jnp.where(side_rows == tall - 1, side, 0.0), axis=0, keepdims=True)
        sent[k + 2, f, 0:16, :] = jnp.broadcast_to(low, (16, channels)).astype(bf16)


def extend(frame, f, tall, wide, got, counts, shifted):
    height, breadth, channels = frame.shape
    row, col = lax.axis_index("row"), lax.axis_index("col")

    def piece(k):
        ok = None
        step = steps[k]
        if step[0] != 0:
            ok = (row > 0) if step[0] > 0 else (row < counts[0] - 1)
        if step[1] != 0:
            ok_col = (col > 0) if step[1] > 0 else (col < counts[1] - 1)
            ok = ok_col if ok is None else jnp.logical_and(ok, ok_col)
        return got[k, f].astype(f32) * jnp.where(ok, 1.0, 0.0)

    below, above = piece(0)[0:breadth], piece(1)[0:breadth]
    right_side, left_side = piece(2), piece(3)
    right_low, left_low = piece(4)[0:1], piece(5)[0:1]
    right_top, left_top = piece(6)[0:1], piece(7)[0:1]
    line_cols = iota3((breadth, channels), 0)
    below = jnp.where(line_cols == wide, right_low, below)
    above = jnp.where(line_cols == wide, right_top, above)
    size = (height + 2) * breadth
    for r in range(height + 2):
        if r == 0:
            line, first = above, left_top
        else:
            if r <= height:
                line = jnp.where(line_cols == wide, right_side[r - 1 : r], frame[r - 1])
                first = left_side[r - 1 : r]
                line = jnp.where(tall + 1 == r, below, line)
                first = jnp.where(tall + 1 == r, left_low, first)
            else:
                line, first = below, left_low
        before = jnp.where(line_cols == 0, first, pltpu.roll(line, 1, 0))
        after = pltpu.roll(line, breadth - 1, 0)
        place = slice(r * breadth, (r + 1) * breadth)
        shifted[f, 0, place, :] = before.astype(bf16)
        shifted[f, 1, place, :] = line.astype(bf16)
        shifted[f, 2, place, :] = after.astype(bf16)


def chunk_of(total):
    for size in (208, 128, 64, 32, 16):
        if total % size == 0:
            return size
    return total


def prior_kernel(
    counts, sizes, cache_one, cache_two, conv_one, conv_two, sum_one, sum_two,
    sent_one, got_one, sent_two, got_two, shifted_one, shifted_two, send_sems, recv_sems,
):
    tall, wide = sizes[0], sizes[1]
    greet([partner(counts, step) for step in steps])
    work = (
        (cache_one, conv_one, sum_one, sent_one, got_one, shifted_one, 1, times),
        (cache_two, conv_two, sum_two, sent_two, got_two, shifted_two, 2, times_t),
    )
    sets = []
    for i, (cache, _, _, sent, got, _, fine, _) in enumerate(work):
        for f in range(2):
            put_pieces(cache[f].astype(f32), f, fine * tall, fine * wide, sent)
        copies = halo_copies(counts, sent, got, send_sems.at[i], recv_sems.at[i])
        for copy in copies:
            copy.start()
        sets.append(copies)
    for copies, (cache, conv, total, sent, got, shifted, fine, product) in zip(sets, work):
        for copy in copies:
            copy.wait()
        for f in range(2):
            extend(cache[f].astype(f32), f, fine * tall, fine * wide, got, counts, shifted)
        breadth = cache.shape[2]
        size = chunk_of(total.shape[0])

        @pl.loop(0, total.shape[0] // size)
        def _(step):
            start = pl.multiple_of(step * size, 16)
            part = jnp.zeros((size, total.shape[1]), f32)
            for f in range(2):
                for a in range(3):
                    for b in range(3):
                        rows = shifted[f, b, pl.ds(start + a * breadth, size), :]
                        part += product(rows, conv[f * 9 + a * 3 + b])
            total[pl.ds(start, size), :] = part


def score_kernel(queries, keys, bias, out):
    scores = times_t(queries[0], keys[...]) + bias[...]
    highest = jnp.max(scores, axis=1, keepdims=True)
    expos = jnp.exp(scores - highest)
    total = jnp.sum(expos, axis=1, keepdims=True)
    mean = times(expos.astype(bf16), keys[...]) / total
    channels = mean.shape[1]
    level = highest + jnp.log(total)
    high = level.astype(bf16).astype(f32)
    mid = (level - high).astype(bf16).astype(f32)
    low = level - high - mid
    lanes = lax.broadcasted_iota(jnp.int32, (mean.shape[0], 128), 1)
    coded = jnp.where(lanes == 0, high, jnp.where(lanes == 1, mid, jnp.where(lanes == 2, low, 0.0)))
    out[0, :, 0:channels] = mean.astype(bf16)
    out[0, :, channels : channels + 128] = coded.astype(bf16)


def tail_kernel(
    counts, sizes, parts, tokens, value_weight, out_weight, gain_one, gain_two,
    sum_one, sum_two, conv_one, conv_two, out,
    got_parts, sent_one, got_one, sent_two, got_two, shifted_one, shifted_two, small, fine_sum,
    part_send, part_recv, send_sems, recv_sems,
):
    row_count = counts[0]
    tall, wide = sizes[0], sizes[1]
    row, col = lax.axis_index("row"), lax.axis_index("col")
    others = [(wrapped(row, d, row_count), col) for d in range(1, row_count)]
    greet(others + [partner(counts, step) for step in steps if step[1] != 0])
    copies = []
    for d, device in enumerate(others):
        copies.append(
            pltpu.make_async_remote_copy(
                src_ref=parts.at[device[0]],
                dst_ref=got_parts.at[d],
                send_sem=part_send.at[d],
                recv_sem=part_recv.at[d],
                device_id=device,
                device_id_type=MESH,
            )
        )
        copies[-1].start()
    for copy in copies:
        copy.wait()
    height, narrow, channels = tokens.shape
    blocks = [parts[row]] + [got_parts[d] for d in range(row_count - 1)]
    levels = [
        jnp.sum(block[:, channels : channels + 128].astype(f32), axis=1, keepdims=True)
        for block in blocks
    ]
    top = functools.reduce(jnp.maximum, levels)
    weights = [jnp.exp(level - top) for level in levels]
    total = functools.reduce(jnp.add, weights)
    mean = functools.reduce(
        jnp.add, [w * block[:, 0:channels].astype(f32) for w, block in zip(weights, blocks)]
    )
    mean = (mean / total).astype(bf16)
    attention = times(mean, value_weight[...]).astype(bf16)
    projected = times(attention, out_weight[...])
    mixed = tokens[...].astype(f32).reshape(height * narrow, channels) + projected
    mixed = mixed.astype(bf16).astype(f32)
    act_one = silu(rms_scale(mixed, gain_one[...])).reshape(height, narrow, channels)
    breadth = small.shape[1]
    small[:, 0:narrow, :] = act_one
    small[:, narrow:breadth, :] = jnp.zeros((height, breadth - narrow, channels), f32)
    frame = small[...]
    put_pieces(frame, 0, tall, wide, sent_one)
    halos = halo_copies(counts, sent_one, got_one, send_sems.at[0], recv_sems.at[0])
    for copy in halos:
        copy.start()
    for copy in halos:
        copy.wait()
    extend(frame, 0, tall, wide, got_one, counts, shifted_one)
    size = height * breadth
    y_one = sum_one[...]
    for a in range(3):
        for b in range(3):
            y_one += times(shifted_one[0, b, a * breadth : a * breadth + size, :], conv_one[a * 3 + b])
    y_one = y_one.astype(bf16).astype(f32)
    frame = silu(rms_scale(y_one, gain_two[...])).reshape(height, breadth, channels)
    put_pieces(frame, 0, tall, wide, sent_two)
    halos = halo_copies(counts, sent_two, got_two, send_sems.at[1], recv_sems.at[1])
    for copy in halos:
        copy.start()
    for copy in halos:
        copy.wait()
    extend(frame, 0, tall, wide, got_two, counts, shifted_two)
    for p in range(2):
        for q in range(2):
            phase = jnp.zeros((size, conv_two.shape[1]), f32)
            for a in range(2):
                for b in range(2):
                    first = (p + a) * breadth
                    phase += times_t(
                        shifted_two[0, q + b, first : first + size, :],
                        conv_two[p * 8 + q * 4 + a * 2 + b],
                    )
            for i in range(height):
                for lane in range(fine_sum.shape[0]):
                    fine_sum[lane, 2 * i + p, pl.ds(q, breadth, stride=2), :] = phase[
                        i * breadth : (i + 1) * breadth, lane * 128 : (lane + 1) * 128
                    ]
    fine_height, fine_narrow, channels_out = out.shape
    fine_breadth = sum_two.shape[1]
    fine_cols = lax.broadcasted_iota(jnp.int32, (fine_narrow, channels_out), 0)
    for i in range(fine_height):
        keep = jnp.logical_and(fine_cols < 2 * wide, i < 2 * tall)
        for lane in range(fine_sum.shape[0]):
            place = slice(lane * 128, min(lane * 128 + 128, channels_out))
            count = place.stop - place.start
            line = fine_sum[lane, i, 0:fine_narrow, 0:count] + sum_two[i, 0:fine_narrow, place]
            out[i, :, place] = jnp.where(keep[:, place], line, 0.0).astype(bf16)


def remote_call(kernel, out_shape, kinds, scratch, number, flops):
    return pl.pallas_call(
        kernel,
        out_shape=out_shape,
        in_specs=[pl.BlockSpec(memory_space=kind) for kind in kinds],
        out_specs=jax.tree.map(lambda _: pl.BlockSpec(memory_space=pltpu.VMEM), out_shape),
        scratch_shapes=scratch,
        compiler_params=pltpu.CompilerParams(
            collective_id=number, has_side_effects=True, vmem_limit_bytes=vmem_bytes
        ),
        cost_estimate=pl.CostEstimate(flops=flops, bytes_accessed=20_000_000, transcendentals=0),
    )


def local(
    counts, tokens, row_sizes, col_sizes, norm_gain, query_weight, key_weight, value_weight,
    out_weight, cache_one, gain_one, conv_one, cache_two, gain_two, conv_two,
):
    height, width, channels = tokens.shape
    channels_out = conv_two.shape[-1]
    rows, cols = counts
    narrow = round_up(width, 8)
    breadth = round_up(width + 1, 16)
    fine_breadth = round_up(2 * width + 1, 16)
    each = height * narrow
    row_count = select_size(row_sizes, lax.axis_index("row"))
    col_count = select_size(col_sizes, lax.axis_index("col"))
    sizes = jnp.stack([row_count, col_count]).astype(jnp.int32)

    padded = jnp.pad(tokens, ((0, 0), (0, narrow - width), (0, 0)))
    normed = rms_scale(padded.astype(f32), norm_gain).astype(bf16).reshape(each, channels)
    queries = times(normed, query_weight).astype(bf16)
    queries = (times_t(queries, key_weight) * (1.0 / math.sqrt(channels))).astype(bf16)
    all_keys = lax.all_gather(normed, "col", axis=0, tiled=True)
    all_queries = lax.all_gather(queries, "row", axis=0)

    wide_one = jnp.pad(cache_one, ((0, 0), (0, 0), (0, breadth - width), (0, 0)))
    wide_two = jnp.pad(cache_two, ((0, 0), (0, 0), (0, fine_breadth - 2 * width), (0, 0)))
    flipped = jnp.swapaxes(conv_two, 3, 4)
    line_one = max(breadth, round_up(height, 16))
    line_two = max(fine_breadth, round_up(2 * height, 16))
    vm = pltpu.VMEM
    sum_one, sum_two = remote_call(
        functools.partial(prior_kernel, counts),
        (
            jax.ShapeDtypeStruct((height * breadth, channels), f32),
            jax.ShapeDtypeStruct((2 * height * fine_breadth, channels_out), f32),
        ),
        [pltpu.SMEM] + [vm] * 4,
        [
            vm((8, 2, line_one, channels), bf16),
            vm((8, 2, line_one, channels), bf16),
            vm((8, 2, line_two, channels), bf16),
            vm((8, 2, line_two, channels), bf16),
            vm((2, 3, (height + 2) * breadth, channels), bf16),
            vm((2, 3, (2 * height + 2) * fine_breadth, channels), bf16),
            pltpu.SemaphoreType.DMA((2, 8)),
            pltpu.SemaphoreType.DMA((2, 8)),
        ],
        1,
        9_000_000_000,
    )(
        sizes,
        wide_one,
        wide_two,
        conv_one[:2].reshape(18, channels, channels),
        flipped[:2].reshape(18, channels_out, channels),
    )
    sum_two = sum_two.reshape(2 * height, fine_breadth, channels_out)

    last = flipped[2].astype(f32)
    by_row = [[last[0], last[1] + last[2]], [last[0] + last[1], last[2]]]
    phases = []
    for p in range(2):
        for q in range(2):
            for a in range(2):
                line = by_row[p][a]
                pair = [line[0], line[1] + line[2]] if q == 0 else [line[0] + line[1], line[2]]
                phases.extend(pair)
    phase_weights = jnp.stack(phases).astype(bf16)
    phase_weights = jnp.pad(phase_weights, ((0, 0), (0, round_up(channels_out, 128) - channels_out), (0, 0)))

    slot_row = lax.broadcasted_iota(jnp.int32, (height, narrow), 0)
    slot_col = lax.broadcasted_iota(jnp.int32, (height, narrow), 1)
    usable = (slot_row < row_count)[None] & (slot_col[None] < col_sizes[:, None, None])
    bias = jnp.where(usable, 0.0, masked_score).astype(f32).reshape(1, cols * each)
    parts = pl.pallas_call(
        score_kernel,
        grid=(rows,),
        out_shape=jax.ShapeDtypeStruct((rows, each, channels + 128), bf16),
        in_specs=[
            pl.BlockSpec((1, each, channels), lambda i: (i, 0, 0)),
            pl.BlockSpec((cols * each, channels), lambda i: (0, 0)),
            pl.BlockSpec((1, cols * each), lambda i: (0, 0)),
        ],
        out_specs=pl.BlockSpec((1, each, channels + 128), lambda i: (i, 0, 0)),
        compiler_params=pltpu.CompilerParams(vmem_limit_bytes=vmem_bytes),
    )(all_queries, all_keys, bias)

    return remote_call(
        functools.partial(tail_kernel, counts),
        jax.ShapeDtypeStruct((2 * height, 2 * width, channels_out), bf16),
        [pltpu.SMEM] + [vm] * 10,
        [
            vm((rows - 1, each, channels + 128), bf16),
            vm((8, 1, line_one, channels), bf16),
            vm((8, 1, line_one, channels), bf16),
            vm((8, 1, line_one, channels), bf16),
            vm((8, 1, line_one, channels), bf16),
            vm((1, 3, (height + 2) * breadth, channels), bf16),
            vm((1, 3, (height + 2) * breadth, channels), bf16),
            vm((height, breadth, channels), f32),
            vm((round_up(channels_out, 128) // 128, 2 * height, 2 * breadth, 128), f32),
            pltpu.SemaphoreType.DMA((rows - 1,)),
            pltpu.SemaphoreType.DMA((rows - 1,)),
            pltpu.SemaphoreType.DMA((2, 8)),
            pltpu.SemaphoreType.DMA((2, 8)),
        ],
        2,
        3_000_000_000,
    )(
        sizes,
        parts,
        padded,
        value_weight,
        out_weight,
        gain_one.reshape(1, channels),
        gain_two.reshape(1, channels),
        sum_one,
        sum_two,
        conv_one[2].reshape(9, channels, channels),
        phase_weights,
    )


def solution(mesh):
    tiled = P("row", "col", None)
    framed = P(None, "row", "col", None)
    placed = (tiled,) + (P(),) * 7 + (framed, P(), P(), framed, P(), P())
    counts = (mesh.shape["row"], mesh.shape["col"])
    return jax.shard_map(
        functools.partial(local, counts),
        mesh=mesh,
        in_specs=placed,
        out_specs=P("row", "col", None),
        check_vma=False,
    )
```

time: 303 us -> 140 us (0.46); the launches traced: 299 us -> 140 us
  waiting for transfers between devices: 117 us -> 0.04 us
  Pallas kernels: 0 us -> 86.1 us
  local copies, waits for them, and re-layouts: 84.9 us -> 18.8 us
  matrix products: 38.6 us -> 0.58 us
  starting transfers between devices: 18.8 us -> 0.01 us
  blocking collectives: 0 us -> 11.5 us
  other arithmetic: 19 us -> 8.91 us
  between operations: 19.9 us -> 13.7 us
    all_gather x2 -> x1, waiting for transfers between devices: 113 us -> 0.02 us  [local(): all_keys = lax.all_gather(normed, 'col', axis=0, tiled=True)]
    pallas_call x0 -> x3, Pallas kernels: none -> 86.1 us  [the longest x1 38.8 us: local(): remote_call(functools.partial(tail_kernel, counts), jax.ShapeDtypeStruct(...]
    unnamed x77 -> x35, local copies, waits for them, and re-layouts: 59.7 us -> 5.17 us
    dot_general x6 -> x1, matrix products: 38.6 us -> 0.58 us  [times_t(): lax.dot_general(left, right, (((1,), (1,)), ((), ())), preferred_element_...]
    ppermute x8 -> x0, starting transfers between devices: 18.8 us -> none  [the longest x4 13.4 us: with_halo(): lax.ppermute(lax.slice_in_dim(block, block.shape[dim] - width, None, axis...]
    all_gather x0 -> x1, blocking collectives: none -> 11.5 us  [local(): all_queries = lax.all_gather(queries, 'row', axis=0)]
    dynamic_update_slice x7 -> x0, local copies, waits for them, and re-layouts: 10.4 us -> none  [the longest x2 5.38 us: settle(): return lax.dynamic_update_slice_in_dim(padded, right_col, col_count + 1, 2)]
    reshape x3 -> x2, local copies, waits for them, and re-layouts: 10.1 us -> 1.14 us  [the longest x1 0.58 us: local(): gain_one.reshape(1, channels)]
  transfers between devices with their start and end apart: 10 -> 1, of which waited for: 5 -> 0; matrix products, arithmetic and copies ran while one was open for 17% -> 15% of each run, Pallas kernels for 0% -> 25%
where the time goes in v1:
time: 140 us
  Pallas kernels  86.1 us (62%)
  local copies, waits for them, and re-layouts  18.8 us (13%)
  between operations  13.7 us (10%)
  blocking collectives  11.5 us (8%)
  other arithmetic  8.91 us (6%)
    pallas_call x1, Pallas kernels, local(): remote_call(functools.partial(tail_kernel, counts), jax.ShapeDtypeStruct(...  38.8 us
    pallas_call x1, Pallas kernels, local(): remote_call(functools.partial(prior_kernel, counts), (jax.ShapeDtypeStruc...  35 us
    pallas_call x1, Pallas kernels, local(): pl.pallas_call(score_kernel, grid=(rows,), out_shape=jax.ShapeDtypeStruct...  12.3 us
    all_gather x1, blocking collectives, local(): all_queries = lax.all_gather(queries, 'row', axis=0)  11.5 us
    unnamed x35, local copies, waits for them, and re-layouts  5.17 us
    slice x1, local copies, waits for them, and re-layouts, local(): conv_one[:2].reshape(18, channels, channels)  2.93 us
  transfers between devices with their start and end apart: 1, of which 0 were waited for; matrix products, arithmetic and copies ran while one was open for 15% of the time, Pallas kernels for 25%

profile of v1, /device:TPU:0, one launch (start us, length us, event | category | flops | bytes accessed | tf_op | source)
XLA Modules:
  0.0 139.6 jit_solution(1396584048705786013)
XLA Ops:
  6.5 0.0 copy-start
  6.5 0.0 all-gather.3.cloned.1.call-start
  6.5 1.1 fusion.4
  7.7 1.8 %fusion.6 = bf16[13,24,384]{2,1,0:T(8,128)(2,1)} fusion(f32[384]{0:T(512)} %param.17, f32[13,24]{1,0:T(8,128)S(1)} %add_rsqrt_fusion, bf16[13,20,384]{2,1,0:T(8,128)(2,1)} %param.14), kind=kLoop, calls=%fused_computation.13 | loop fusion | flops 479232 | bytes 442080 | tf_op jit(solution)/shard_map/convert_element_type | solution.py:327
  9.4 0.0 all-gather.3.cloned.1.call-update
  9.5 1.9 %slice_convert_fusion = (f32[1,3,3,192,384]{4,3,2,1,0:T(8,128)S(1)}, f32[3,3,192,384]{3,2,1,0:T(8,128)S(1)}) fusion(bf16[3,3,3,192,384]{4,3,2,1,0:T(8,128)(2,1)} %bitcast.85), kind=kLoop, calls=%fused_computation | loop fusion | flops 663552 | bytes 6635520 | tf_op jit(solution)/shard_map/convert_element_type | solution.py:367
  11.4 0.0 slice-start
  11.4 0.1 fusion.1
  11.6 0.0 copy-start.1
  11.8 0.0 slice-start.1
  12.0 1.9 %copy-done.1 = bf16[3,3,3,384,192]{3,4,2,1,0:T(8,128)(2,1)S(1)} copy-done((bf16[3,3,3,384,192]{3,4,2,1,0:T(8,128)(2,1)S(1)}, bf16[3,3,3,384,192]{3,4,2,1,0:T(8,128)(2,1)}, u32[]{:S(2)}) %copy-start.1) | copy-done | bytes 3981336
  13.9 1.9 %slice.136 = bf16[2,3,3,192,384]{4,3,2,1,0:T(8,128)(2,1)} slice(bf16[3,3,3,192,384]{4,3,2,1,0:T(8,128)(2,1)S(1)} %bitcast.86), slice={[0:2], [0:3], [0:3], [0:192], [0:384]} | slice | bytes 5308416 | tf_op jit(solution)/shard_map/slice | solution.py:363
  15.8 0.0 slice-done
  15.8 1.1 slice-done.1
  16.8 2.9 %slice.109 = bf16[2,3,3,384,384]{4,3,2,1,0:T(8,128)(2,1)} slice(bf16[3,3,3,384,384]{4,3,2,1,0:T(8,128)(2,1)S(1)} %bitcast.83), slice={[0:2], [0:3], [0:3], [0:384], [0:384]} | slice | bytes 10616832 | tf_op jit(solution)/shard_map/slice | solution.py:362
  19.8 1.9 %slice.111 = bf16[1,3,3,384,384]{4,3,2,1,0:T(8,128)(2,1)} slice(bf16[3,3,3,384,384]{4,3,2,1,0:T(8,128)(2,1)S(1)} %bitcast.83), slice={[2:3], [0:3], [0:3], [0:384], [0:384]} | slice | bytes 5308416 | tf_op jit(solution)/shard_map/slice | solution.py:427
  21.7 0.0 copy-done.2
  21.7 0.7 pad.16.tokens
  22.6 0.0 copy-start.3
  22.6 2.1 %pad.19.conv_two = bf16[16,256,384]{2,1,0:T(8,128)(2,1)} pad(bf16[16,192,384]{2,1,0:T(8,128)(2,1)S(1)} %fusion.22, bf16[]{:T(256)} %constant.8.clone.1), padding=0_0x0_64x0_0 | pad | bytes 5505026 | tf_op jit(solution)/shard_map/jit(_pad)/pad | solution.py:377
  24.6 0.0 copy-done.3
  24.7 0.0 copy-start.6
  24.7 0.0 copy-start.7
  24.7 0.0 copy-start.4
  24.7 0.0 copy-start.9
  24.7 1.4 %pad.18.cache_two = bf16[2,26,48,384]{3,2,1,0:T(8,128)(2,1)} pad(bf16[2,26,40,384]{3,2,1,0:T(8,128)(2,1)S(1)} %copy-done.3, bf16[]{:T(256)} %constant.8.clone.1), padding=0_0x0_0x0_8x0_0 | pad | bytes 3514370 | tf_op jit(solution)/shard_map/jit(_pad)/pad | solution.py:334
  26.1 0.0 copy-done.5
  26.1 0.1 copy.16
  26.2 0.9 pad.17.cache_one
  27.1 0.0 copy-done.10
  27.1 0.6 fusion.41
  27.7 0.6 iota_compare_fusion.1
  28.3 0.0 copy-done.8
  28.3 0.1 fusion.40
  28.4 0.7 select_n.25.bias
  29.1 0.0 copy-done.6
  29.1 0.6 reshape.165.gain_one
  29.7 0.6 reshape.166.gain_two
  30.3 0.6 fusion.42
  30.9 1.8 %pad_add_fusion.sizes = s32[2]{0:T(128)} fusion(s32[1]{0:T(128)} %bitcast.1, s32[1]{0:T(128)} %bitcast), kind=kLoop, calls=%fused_computation.70 | loop fusion | flops 2 | bytes 16 | tf_op jit(solution)/shard_map/stack | solution.py:324
  32.7 0.0 copy-done
  32.7 0.6 fusion
  33.3 11.5 %all-gather = bf16[1248,384]{1,0:T(8,128)(2,1)} all-gather(bf16[312,384]{1,0:T(8,128)(2,1)S(1)} %fusion), channel_id=2, replica_groups=mesh['row'=4,'col'=8] {'row'}, dimensions={0}, use_global_device_ids=true | all-gather | bytes 1198080 | tf_op jit(solution)/shard_map/all_gather | solution.py:331
  44.7 35.0 %shard_map.137 = (f32[416,384]{1,0:T(8,128)}, f32[1248,192]{1,0:T(8,128)}) custom-call(s32[2]{0:T(128)} %pad_add_fusion.sizes, bf16[2,13,32,384]{3,2,1,0:T(8,128)(2,1)} %pad.17.cache_one, bf16[2,26,48,384]{3,2,1,0:T(8,128)(2,1)} %pad.18.cache_two, bf16[18,384,384]{2,1,0:T(8,128)(2,1)} %bitcast.84, bf16[18,192,384]{2,1,0:T(8,128)(2,1)} %bitcast.89), custom_call_target="tpu_custom_call" | custom-call | flops 8999999488 | bytes 20000000 | tf_op jit(solution)/shard_map/pallas_call | solution.py:339
  79.8 0.0 all-gather.3.cloned.1.call-done.keys
  79.8 12.3 %shard_map.136.parts = bf16[4,312,512]{2,1,0:T(8,128)(2,1)} custom-call(bf16[4,312,384]{2,1,0:T(8,128)(2,1)} %bitcast.87, bf16[2496,384]{1,0:T(8,128)(2,1)} %all-gather.3.cloned.1.call-done.keys, f32[1,2496]{1,0:T(1,128)} %select_n.25.bias), custom_call_target="tpu_custom_call" | custom-call | tf_op jit(solution)/shard_map/pallas_call | solution.py:383
  92.1 38.8 %shard_map.138 = bf16[26,40,192]{2,1,0:T(8,128)(2,1)} custom-call(s32[2]{0:T(128)} %pad_add_fusion.sizes, bf16[4,312,512]{2,1,0:T(8,128)(2,1)} %shard_map.136.parts, bf16[13,24,384]{2,1,0:T(8,128)(2,1)} %pad.16.tokens, bf16[384,384]{1,0:T(8,128)(2,1)} %value_weight.1, bf16[384,384]{1,0:T(8,128)(2,1)} %out_weight.1, f32[1,384]{1,0:T(1,128)} %reshape.165.gain_one, ...), custom_call_target="tpu_custom_call" | custom-call | flops 3000000000 | bytes 20000000 | tf_op jit(solution)/shard_map/pallas_call | solution.py:396
  130.9 1.9 %copy.33 = bf16[26,40,192]{2,1,0:T(8,128)(2,1)} copy(bf16[26,40,192]{2,1,0:T(8,128)(2,1)} %shard_map.138) | data formatting | bytes 798720
  (25 shorter events, 0.6 us)
Async XLA Ops:
  6.5 26.1 %copy-start = (bf16[384,384]{1,0:T(8,128)(2,1)S(1)}, bf16[384,384]{1,0:T(8,128)(2,1)}, u32[]{:S(2)}) copy-start(bf16[384,384]{1,0:T(8,128)(2,1)} %param.19) | copy-start | bytes 884740
  6.5 73.3 %all-gather.3.cloned.1.call-start = ((), (), s32[]{:S(2)}) async-start(), calls=%async_computation | async-start | bytes 2156544 | tf_op jit(solution)/shard_map/all_gather | solution.py:330
  11.4 4.4 %slice-start = ((s8[7962624]{0:T(1024)(128)(4,1)}), s8[3768320]{0:T(1024)(128)(4,1)S(1)}, s32[]{:S(2)}) async-start(s8[7962624]{0:T(1024)(128)(4,1)} %bitcast.82), calls=%async_computation.1 | async-start | bytes 7536640
  11.6 2.3 %copy-start.1 = (bf16[3,3,3,384,192]{3,4,2,1,0:T(8,128)(2,1)S(1)}, bf16[3,3,3,384,192]{3,4,2,1,0:T(8,128)(2,1)}, u32[]{:S(2)}) copy-start(bf16[3,3,3,384,192]{3,4,2,1,0:T(8,128)(2,1)} %param.27) | copy-start | bytes 11943940
  11.8 5.1 %slice-start.1 = ((s8[7962624]{0:T(1024)(128)(4,1)}), s8[4194304]{0:T(1024)(128)(4,1)S(1)}, s32[]{:S(2)}) async-start(s8[7962624]{0:T(1024)(128)(4,1)} %bitcast.82), calls=%async_computation.2 | async-start | bytes 8388608
  19.8 1.9 %copy-start.2 = (bf16[13,20,384]{2,1,0:T(8,128)(2,1)S(1)}, bf16[13,20,384]{2,1,0:T(8,128)(2,1)}, u32[]{:S(2)}) copy-start(bf16[13,20,384]{2,1,0:T(8,128)(2,1)} %param.14) | copy-start | bytes 599044
  22.6 2.1 %copy-start.3 = (bf16[2,26,40,384]{3,2,1,0:T(8,128)(2,1)S(1)}, bf16[2,26,40,384]{3,2,1,0:T(8,128)(2,1)}, u32[]{:S(2)}) copy-start(bf16[2,26,40,384]{3,2,1,0:T(8,128)(2,1)} %param.25) | copy-start | bytes 4792324
  24.6 1.5 %copy-start.5 = (bf16[2,13,20,384]{3,0,2,1:T(2,128)(2,1)S(1)}, bf16[2,13,20,384]{3,0,2,1:T(2,128)(2,1)}, u32[]{:S(2)}) copy-start(bf16[2,13,20,384]{3,0,2,1:T(2,128)(2,1)} %param.22) | copy-start | bytes 1198084
  24.7 2.5 %copy-start.10 = (s32[4]{0:T(128)S(1)}, s32[4]{0:T(128)}, u32[]{:S(2)}) copy-start(s32[4]{0:T(128)} %param.15) | copy-start | bytes 52
  24.7 3.7 %copy-start.8 = (s32[8]{0:T(128)S(1)}, s32[8]{0:T(128)}, u32[]{:S(2)}) copy-start(s32[8]{0:T(128)} %param.16) | copy-start | bytes 100
  24.7 4.5 %copy-start.6 = (f32[384]{0:T(512)S(1)}, f32[384]{0:T(512)}, u32[]{:S(2)}) copy-start(f32[384]{0:T(512)} %param.23) | copy-start | bytes 4612
  24.7 5.0 %copy-start.7 = (f32[384]{0:T(512)S(1)}, f32[384]{0:T(512)}, u32[]{:S(2)}) copy-start(f32[384]{0:T(512)} %param.26) | copy-start | bytes 4612
  24.7 8.0 %copy-start.4 = (bf16[13,24,384]{2,1,0:T(8,128)(2,1)S(1)}, bf16[13,24,384]{2,1,0:T(8,128)(2,1)}, u32[]{:S(2)}) copy-start(bf16[13,24,384]{2,1,0:T(8,128)(2,1)} %fusion.6) | copy-start | bytes 718852
  24.7 8.0 %copy-start.9 = (bf16[384,384]{1,0:T(8,128)(2,1)S(1)}, bf16[384,384]{1,0:T(8,128)(2,1)}, u32[]{:S(2)}) copy-start(bf16[384,384]{1,0:T(8,128)(2,1)} %param.18) | copy-start | bytes 884740
Sparse Core Ops, SparseCore 0:
  9.6 52.6 all-gather.2

commit v2 on v1

v2 whole, which is shorter than its diff:
```python
import functools
import math

import jax
import jax.numpy as jnp
from jax import lax
from jax.experimental import pallas as pl
from jax.experimental.pallas import tpu as pltpu
from jax.sharding import PartitionSpec as P

epsilon = 1e-06
masked_score = -1e30
f32 = jnp.float32
bf16 = jnp.bfloat16
MESH = pl.DeviceIdType.MESH
steps = ((-1, 0), (1, 0), (0, -1), (0, 1), (-1, -1), (-1, 1), (1, -1), (1, 1))
vmem_bytes = 58 * 1024 * 1024


def round_up(value, unit):
    return -(-value // unit) * unit


def rms_scale(wide, gain_vec):
    return wide * lax.rsqrt(jnp.mean(wide * wide, axis=-1, keepdims=True) + epsilon) * gain_vec


def silu(wide):
    return wide / (1.0 + jnp.exp(-wide))


def times(left, right):
    return jnp.dot(left, right, preferred_element_type=f32)


def times_t(left, right):
    return lax.dot_general(left, right, (((1,), (1,)), ((), ())), preferred_element_type=f32)


def wrapped(position, step, count):
    return lax.rem(position + step + count, count)


def partner(counts, step):
    return (
        wrapped(lax.axis_index("row"), step[0], counts[0]),
        wrapped(lax.axis_index("col"), step[1], counts[1]),
    )


def greet(devices):
    barrier = pltpu.get_barrier_semaphore()
    for device in devices:
        pl.semaphore_signal(barrier, inc=1, device_id=device, device_id_type=MESH)
    pl.semaphore_wait(barrier, len(devices))


def iota3(shape, dim):
    return lax.broadcasted_iota(jnp.int32, shape, dim)


def halo_copies(counts, sent, got, send_sems, recv_sems):
    return [
        pltpu.make_async_remote_copy(
            src_ref=sent.at[k],
            dst_ref=got.at[k],
            send_sem=send_sems.at[k],
            recv_sem=recv_sems.at[k],
            device_id=partner(counts, step),
            device_id_type=MESH,
        )
        for k, step in enumerate(steps)
    ]


def put_pieces(frame, last_line, f, tall, wide, sent):
    height, breadth, channels = frame.shape
    cols = iota3(frame.shape, 1)
    left = jnp.concatenate([frame[r, 0:1, :] for r in range(height)], axis=0)
    right = jnp.sum(jnp.where(cols == wide - 1, frame, 0.0), axis=1)
    side_rows = iota3(left.shape, 0)
    sent[0, f, 0:breadth, :] = frame[0].astype(bf16)
    sent[1, f, 0:breadth, :] = last_line.astype(bf16)
    sent[2, f, 0:height, :] = left.astype(bf16)
    sent[3, f, 0:height, :] = right.astype(bf16)
    for k, side in ((4, left), (5, right)):
        sent[k, f, 0:16, :] = jnp.broadcast_to(side[0:1], (16, channels)).astype(bf16)
        low = jnp.sum(jnp.where(side_rows == tall - 1, side, 0.0), axis=0, keepdims=True)
        sent[k + 2, f, 0:16, :] = jnp.broadcast_to(low, (16, channels)).astype(bf16)


def extend(frame, f, tall, wide, got, counts, shifted):
    height, breadth, channels = frame.shape
    row, col = lax.axis_index("row"), lax.axis_index("col")

    def piece(k):
        ok = None
        step = steps[k]
        if step[0] != 0:
            ok = (row > 0) if step[0] > 0 else (row < counts[0] - 1)
        if step[1] != 0:
            ok_col = (col > 0) if step[1] > 0 else (col < counts[1] - 1)
            ok = ok_col if ok is None else jnp.logical_and(ok, ok_col)
        return got[k, f].astype(f32) * jnp.where(ok, 1.0, 0.0)

    below, above = piece(0)[0:breadth], piece(1)[0:breadth]
    right_side, left_side = piece(2), piece(3)
    right_low, left_low = piece(4)[0:1], piece(5)[0:1]
    right_top, left_top = piece(6)[0:1], piece(7)[0:1]
    line_cols = iota3((breadth, channels), 0)
    below = jnp.where(line_cols == wide, right_low, below)
    above = jnp.where(line_cols == wide, right_top, above)
    size = (height + 2) * breadth
    for r in range(height + 2):
        if r == 0:
            line, first = above, left_top
        else:
            if r <= height:
                line = jnp.where(line_cols == wide, right_side[r - 1 : r], frame[r - 1])
                first = left_side[r - 1 : r]
                line = jnp.where(tall + 1 == r, below, line)
                first = jnp.where(tall + 1 == r, left_low, first)
            else:
                line, first = below, left_low
        before = jnp.where(line_cols == 0, first, pltpu.roll(line, 1, 0))
        after = pltpu.roll(line, breadth - 1, 0)
        place = slice(r * breadth, (r + 1) * breadth)
        shifted[f, 0, place, :] = before.astype(bf16)
        shifted[f, 1, place, :] = line.astype(bf16)
        shifted[f, 2, place, :] = after.astype(bf16)


def widened(frame, breadth):
    frame = frame.astype(f32)
    gap = breadth - frame.shape[-2]
    if gap == 0:
        return frame
    zeros = jnp.zeros(frame.shape[:-2] + (gap, frame.shape[-1]), f32)
    return jnp.concatenate([frame, zeros], axis=-2)


def key_spread(counts, keys, sems):
    fwd_sems, bwd_sems, fast_sems, recv_sems = sems
    cols = counts[1]
    fast = fast_part(cols)
    slow = cols // fast
    row, col = lax.axis_index("row"), lax.axis_index("col")
    s, f = col // fast, col % fast

    def copy_to(block, sem, slow_at, fast_at):
        return pltpu.make_async_remote_copy(
            src_ref=keys.at[block],
            dst_ref=keys.at[block],
            send_sem=sem,
            recv_sem=recv_sems.at[block],
            device_id=(row, slow_at * fast + fast_at),
            device_id_type=MESH,
        )

    def fast_copies(block_s):
        return [
            copy_to(block_s * fast + f, fast_sems.at[d - 1, block_s], s, (f + d) % fast)
            for d in range(1, fast)
        ]

    def line_copy(hop, up):
        block_s = s - hop if up else s + hop
        sems_at = fwd_sems if up else bwd_sems
        return copy_to(block_s * fast + f, sems_at.at[hop], s + 1 if up else s - 1, f)

    def goes(hop, up):
        if up:
            return jnp.logical_and(s - hop >= 0, s + 1 < slow)
        return jnp.logical_and(s + hop < slow, s - 1 >= 0)

    def start():
        for up in (True, False):
            @pl.when(goes(0, up))
            def _():
                line_copy(0, up).start()

        for copy in fast_copies(s):
            copy.start()

    def hop(step):
        for up in (True, False):
            came = (s - step >= 0) if up else (s + step < slow)

            @pl.when(came)
            def _():
                block_s = s - step if up else s + step
                copy_to(block_s * fast + f, fwd_sems.at[0], s, f).wait_recv()
                for copy in fast_copies(block_s):
                    copy.start()

            if step < slow - 1:
                @pl.when(goes(step, up))
                def _():
                    line_copy(step, up).start()

    def finish():
        for block_s in range(slow):
            for d in range(1, fast):
                copy_to(block_s * fast + (f + d) % fast, fwd_sems.at[0], s, f).wait_recv()
            for copy in fast_copies(block_s):
                copy.wait_send()
        for step in range(slow - 1):
            for up in (True, False):
                @pl.when(goes(step, up))
                def _():
                    line_copy(step, up).wait_send()

    greeted = [(row, s * fast + (f + d) % fast) for d in range(1, fast)]
    return start, hop, finish, greeted, slow


def fast_part(cols):
    fast = 1 << ((cols.bit_length() - 1) // 2)
    return fast if cols % fast == 0 else 1


def convolve_rows(shifted, frames, conv, product, start, size, breadth):
    part = None
    for f in range(frames):
        for a in range(3):
            for b in range(3):
                rows = shifted[f, b, start + a * breadth : start + a * breadth + size, :]
                term = product(rows, conv[f * 9 + a * 3 + b])
                part = term if part is None else part + term
    return part


def prior_kernel(
    counts, row_sizes, col_sizes, tokens, norm_gain, query_weight, key_weight,
    cache_one, cache_two, conv_one, conv_two,
    sum_one, sum_two, keys, queries, phase_weights,
    sent_one, got_one, sent_two, got_two, shifted_one, shifted_two, held_one, held_two,
    send_sems, recv_sems, query_send, query_recv, fwd_sems, bwd_sems, fast_sems, key_recv, load_sems,
):
    row_count, col_count = counts
    row, col = lax.axis_index("row"), lax.axis_index("col")
    tall, wide = row_sizes[row], col_sizes[col]
    loads = [
        pltpu.make_async_copy(conv_two, held_two, load_sems.at[0]),
        pltpu.make_async_copy(conv_one.at[0:18], held_one, load_sems.at[1]),
    ]
    for load in loads:
        load.start()
    key_sems = (fwd_sems, bwd_sems, fast_sems, key_recv)
    start, hop, finish, fast_others, slow = key_spread(counts, keys, key_sems)
    fast = col_count // slow
    line = [
        (row, wrapped(col, step * fast, col_count)) for step in ((1, -1) if slow > 1 else ())
    ]
    others = [(wrapped(row, d, row_count), col) for d in range(1, row_count)]
    greet(
        others + fast_others + line
        + [partner(counts, step) for step in steps if step[1] != 0]
    )
    normed = rms_scale(tokens[...].astype(f32), norm_gain[...][None, :]).astype(bf16)
    keys[col] = normed
    start()
    query = times(normed, query_weight[...]).astype(bf16)
    unit = math.log2(math.e) / math.sqrt(tokens.shape[1])
    queries[row] = (times_t(query, key_weight[...]) * unit).astype(bf16)
    query_copies = [
        pltpu.make_async_remote_copy(
            src_ref=queries.at[row],
            dst_ref=queries.at[row],
            send_sem=query_send.at[d],
            recv_sem=query_recv.at[d],
            device_id=device,
            device_id_type=MESH,
        )
        for d, device in enumerate(others)
    ]
    for copy in query_copies:
        copy.start()
    breadth, fine_breadth = cache_one.shape[2], round_up(cache_two.shape[2] + 1, 16)
    for f in range(2):
        last_line = cache_one[f, jnp.maximum(tall, 1) - 1].astype(f32)
        put_pieces(cache_one[f].astype(f32), last_line, f, tall, wide, sent_one)
    halos_one = halo_copies(counts, sent_one, got_one, send_sems.at[0], recv_sems.at[0])
    for copy in halos_one:
        copy.start()
    for f in range(2):
        last_line = widened(cache_two[f, 2 * jnp.maximum(tall, 1) - 1], fine_breadth)
        frame = widened(cache_two[f], fine_breadth)
        put_pieces(frame, last_line, f, 2 * tall, 2 * wide, sent_two)
    halos_two = halo_copies(counts, sent_two, got_two, send_sems.at[1], recv_sems.at[1])
    for copy in halos_two:
        copy.start()
    if slow > 1:
        hop(1)
    loads[0].wait()
    channels_out = held_two.shape[1]
    phase_weights[:, channels_out:, :] = jnp.zeros_like(phase_weights[:, channels_out:, :])
    for p in range(2):
        for q in range(2):
            for a in range(2):
                for b in range(2):
                    rows_in = ((0,), (1, 2))[a] if p == 0 else ((0, 1), (2,))[a]
                    cols_in = ((0,), (1, 2))[b] if q == 0 else ((0, 1), (2,))[b]
                    taps = [held_two[18 + 3 * i + j].astype(f32) for i in rows_in for j in cols_in]
                    total = functools.reduce(jnp.add, taps).astype(bf16)
                    phase_weights[p * 8 + q * 4 + a * 2 + b, 0:channels_out, :] = total
    for copy in halos_one:
        copy.wait()
    for f in range(2):
        extend(cache_one[f].astype(f32), f, tall, wide, got_one, counts, shifted_one)
    if slow > 2:
        hop(2)
    loads[1].wait()
    sum_one[...] = convolve_rows(
        shifted_one, 2, held_one, times, 0, sum_one.shape[0], breadth
    )
    for step in range(3, slow):
        hop(step)
    for copy in halos_two:
        copy.wait()
    for f in range(2):
        frame = widened(cache_two[f], fine_breadth)
        extend(frame, f, 2 * tall, 2 * wide, got_two, counts, shifted_two)
    total = sum_two.shape[0]
    size = total // 3 if total % 48 == 0 else total
    for at in range(0, total, size):
        sum_two[at : at + size, :] = convolve_rows(
            shifted_two, 2, held_two, times_t, at, size, fine_breadth
        )
    finish()
    for copy in query_copies:
        copy.wait()


def tail_kernel(
    counts, width, row_sizes, col_sizes, queries, keys, tokens, value_weight, out_weight,
    gain_one, gain_two, sum_one, sum_two, conv_two, conv_one, out,
    parts, bias, held_one, got_parts, sent_one, got_one, sent_two, got_two,
    shifted_one, shifted_two, flat, small, fine_sum,
    part_send, part_recv, send_sems, recv_sems, load_sem,
):
    row_count, col_count = counts
    row, col = lax.axis_index("row"), lax.axis_index("col")
    tall, wide = row_sizes[row], col_sizes[col]
    load = pltpu.make_async_copy(conv_one.at[18:27], held_one, load_sem)
    load.start()
    others = [(wrapped(row, d, row_count), col) for d in range(1, row_count)]
    greet(others + [partner(counts, step) for step in steps if step[1] != 0])
    each, channels = tokens.shape
    height, breadth, _ = small.shape
    slot = lax.broadcasted_iota(jnp.int32, (1, each), 1)
    slot_row = jnp.zeros((1, each), jnp.int32)
    for r in range(1, height + 1):
        slot_row += jnp.where(slot >= r * width, 1, 0)
    slot_col = slot - slot_row * width
    for c in range(col_count):
        usable = jnp.logical_and(slot_row < tall, slot_col < col_sizes[c])
        bias[c : c + 1, :] = jnp.where(usable, 0.0, masked_score)
    masks = jnp.concatenate([bias[c : c + 1, :] for c in range(col_count)], axis=1)
    lanes = lax.broadcasted_iota(jnp.int32, (each, 128), 1)

    def partial_of(target):
        all_keys = keys[...].reshape(col_count * each, channels)
        scores = times_t(queries[target], all_keys) + masks
        highest = jnp.max(scores, axis=1, keepdims=True)
        expos = jnp.exp2(scores - highest)
        total = jnp.sum(expos, axis=1, keepdims=True)
        mean = times(expos.astype(bf16), all_keys) / total
        level = highest + jnp.log2(total)
        high = level.astype(bf16).astype(f32)
        mid = (level - high).astype(bf16).astype(f32)
        low = level - high - mid
        coded = jnp.where(lanes == 0, high, jnp.where(lanes == 1, mid, jnp.where(lanes == 2, low, 0.0)))
        parts[target, :, 0:channels] = mean.astype(bf16)
        parts[target, :, channels : channels + 128] = coded.astype(bf16)

    copies = []
    for d in sorted(range(1, row_count), key=lambda d: -min(d, row_count - d)):
        target = others[d - 1][0]
        partial_of(target)
        copies.append(
            pltpu.make_async_remote_copy(
                src_ref=parts.at[target],
                dst_ref=got_parts.at[d - 1],
                send_sem=part_send.at[d - 1],
                recv_sem=part_recv.at[d - 1],
                device_id=others[d - 1],
                device_id_type=MESH,
            )
        )
        copies[-1].start()
    partial_of(row)
    for copy in copies:
        copy.wait()
    blocks = [parts[row]] + [got_parts[d] for d in range(row_count - 1)]
    levels = [
        jnp.sum(block[:, channels : channels + 128].astype(f32), axis=1, keepdims=True)
        for block in blocks
    ]
    top = functools.reduce(jnp.maximum, levels)
    weights = [jnp.exp2(level - top) for level in levels]
    total = functools.reduce(jnp.add, weights)
    mean = functools.reduce(
        jnp.add, [w * block[:, 0:channels].astype(f32) for w, block in zip(weights, blocks)]
    )
    mean = (mean / total).astype(bf16)
    attention = times(mean, value_weight[...]).astype(bf16)
    projected = times(attention, out_weight[...])
    mixed = (tokens[...].astype(f32) + projected).astype(bf16).astype(f32)
    flat[...] = silu(rms_scale(mixed, gain_one[...][None, :]))
    small[...] = jnp.zeros_like(small)
    for r in range(height):
        small[r, 0:width, :] = flat[r * width : (r + 1) * width, :]
    frame = small[...]
    put_pieces(frame, small[jnp.maximum(tall, 1) - 1], 0, tall, wide, sent_one)
    halos = halo_copies(counts, sent_one, got_one, send_sems.at[0], recv_sems.at[0])
    for copy in halos:
        copy.start()
    load.wait()
    for copy in halos:
        copy.wait()
    extend(frame, 0, tall, wide, got_one, counts, shifted_one)
    size = height * breadth
    y_one = sum_one[...] + convolve_rows(shifted_one, 1, held_one, times, 0, size, breadth)
    y_one = y_one.astype(bf16).astype(f32)
    small[...] = silu(rms_scale(y_one, gain_two[...][None, :])).reshape(height, breadth, channels)
    frame = small[...]
    put_pieces(frame, small[jnp.maximum(tall, 1) - 1], 0, tall, wide, sent_two)
    halos = halo_copies(counts, sent_two, got_two, send_sems.at[1], recv_sems.at[1])
    for copy in halos:
        copy.start()
    for copy in halos:
        copy.wait()
    extend(frame, 0, tall, wide, got_two, counts, shifted_two)
    for p in range(2):
        for q in range(2):
            phase = jnp.zeros((size, conv_two.shape[1]), f32)
            for a in range(2):
                for b in range(2):
                    first = (p + a) * breadth
                    phase += times_t(
                        shifted_two[0, q + b, first : first + size, :],
                        conv_two[p * 8 + q * 4 + a * 2 + b],
                    )
            for i in range(height):
                for lane in range(fine_sum.shape[0]):
                    fine_sum[lane, 2 * i + p, pl.ds(q, breadth, stride=2), :] = phase[
                        i * breadth : (i + 1) * breadth, lane * 128 : (lane + 1) * 128
                    ]
    fine_height, fine_narrow, channels_out = out.shape
    fine_breadth = sum_two.shape[1]
    fine_cols = lax.broadcasted_iota(jnp.int32, (fine_narrow, channels_out), 0)
    for i in range(fine_height):
        keep = jnp.logical_and(fine_cols < 2 * wide, i < 2 * tall)
        for lane in range(fine_sum.shape[0]):
            place = slice(lane * 128, min(lane * 128 + 128, channels_out))
            count = place.stop - place.start
            line = fine_sum[lane, i, 0:fine_narrow, 0:count] + sum_two[i, 0:fine_narrow, place]
            out[i, :, place] = jnp.where(keep[:, place], line, 0.0).astype(bf16)


def remote_call(kernel, out_shape, kinds, scratch, number, flops):
    return pl.pallas_call(
        kernel,
        out_shape=out_shape,
        in_specs=[pl.BlockSpec(memory_space=kind) for kind in kinds],
        out_specs=jax.tree.map(lambda _: pl.BlockSpec(memory_space=pltpu.VMEM), out_shape),
        scratch_shapes=scratch,
        compiler_params=pltpu.CompilerParams(
            collective_id=number, has_side_effects=True, vmem_limit_bytes=vmem_bytes
        ),
        cost_estimate=pl.CostEstimate(flops=flops, bytes_accessed=20_000_000, transcendentals=0),
    )


def local(
    counts, tokens, row_sizes, col_sizes, norm_gain, query_weight, key_weight, value_weight,
    out_weight, cache_one, gain_one, conv_one, cache_two, gain_two, conv_two,
):
    height, width, channels = tokens.shape
    channels_out = conv_two.shape[-1]
    rows, cols = counts
    breadth = round_up(width + 1, 16)
    fine_breadth = round_up(2 * width + 1, 16)
    each = round_up(height * width, 16)

    flat = jnp.pad(tokens.reshape(height * width, channels), ((0, each - height * width), (0, 0)))
    wide_one = jnp.pad(cache_one, ((0, 0), (0, 0), (0, breadth - width), (0, 0)))
    kernels_one = conv_one.reshape(27, channels, channels)
    kernels_two = jnp.swapaxes(conv_two, 3, 4).reshape(27, channels_out, channels)
    line_one = max(breadth, round_up(height, 16))
    line_two = max(fine_breadth, round_up(2 * height, 16))
    lanes_out = round_up(channels_out, 128)
    fast = fast_part(cols)
    slow = cols // fast
    vm, sm, dma = pltpu.VMEM, pltpu.SMEM, pltpu.SemaphoreType.DMA
    shape = jax.ShapeDtypeStruct
    sum_one, sum_two, keys, queries, phase_weights = remote_call(
        functools.partial(prior_kernel, counts),
        (
            shape((height * breadth, channels), f32),
            shape((2 * height * fine_breadth, channels_out), f32),
            shape((cols, each, channels), bf16),
            shape((rows, each, channels), bf16),
            shape((16, lanes_out, channels), bf16),
        ),
        [sm] * 2 + [vm] * 6 + [pl.ANY] * 2,
        [
            vm((8, 2, line_one, channels), bf16),
            vm((8, 2, line_one, channels), bf16),
            vm((8, 2, line_two, channels), bf16),
            vm((8, 2, line_two, channels), bf16),
            vm((2, 3, (height + 2) * breadth, channels), bf16),
            vm((2, 3, (2 * height + 2) * fine_breadth, channels), bf16),
            vm((18, channels, channels), bf16),
            vm((27, channels_out, channels), bf16),
            dma((2, 8)),
            dma((2, 8)),
            dma((rows - 1,)),
            dma((rows - 1,)),
            dma((slow,)),
            dma((slow,)),
            dma((max(fast - 1, 1), slow)),
            dma((cols,)),
            dma((2,)),
        ],
        1,
        9_000_000_000,
    )(
        row_sizes, col_sizes, flat, norm_gain, query_weight, key_weight,
        wide_one, cache_two, kernels_one, kernels_two,
    )
    sum_two = sum_two.reshape(2 * height, fine_breadth, channels_out)
    return remote_call(
        functools.partial(tail_kernel, counts, width),
        shape((2 * height, 2 * width, channels_out), bf16),
        [sm] * 2 + [vm] * 10 + [pl.ANY],
        [
            vm((rows, each, channels + 128), bf16),
            vm((round_up(cols, 8), each), f32),
            vm((9, channels, channels), bf16),
            vm((rows - 1, each, channels + 128), bf16),
            vm((8, 1, line_one, channels), bf16),
            vm((8, 1, line_one, channels), bf16),
            vm((8, 1, line_one, channels), bf16),
            vm((8, 1, line_one, channels), bf16),
            vm((1, 3, (height + 2) * breadth, channels), bf16),
            vm((1, 3, (height + 2) * breadth, channels), bf16),
            vm((each, channels), f32),
            vm((height, breadth, channels), f32),
            vm((lanes_out // 128, 2 * height, 2 * breadth, 128), f32),
            dma((rows - 1,)),
            dma((rows - 1,)),
            dma((2, 8)),
            dma((2, 8)),
            dma,
        ],
        2,
        9_000_000_000,
    )(
        row_sizes, col_sizes, queries, keys, flat, value_weight, out_weight,
        gain_one, gain_two, sum_one, sum_two, phase_weights, kernels_one,
    )


def solution(mesh):
    tiled = P("row", "col", None)
    framed = P(None, "row", "col", None)
    placed = (tiled,) + (P(),) * 7 + (framed, P(), P(), framed, P(), P())
    counts = (mesh.shape["row"], mesh.shape["col"])
    return jax.shard_map(
        functools.partial(local, counts),
        mesh=mesh,
        in_specs=placed,
        out_specs=P("row", "col", None),
        check_vma=False,
    )
```

time: 140 us -> 91.2 us (0.65)
  between operations: 13.7 us -> 0.02 us
  local copies, waits for them, and re-layouts: 18.8 us -> 5.53 us
  blocking collectives: 11.5 us -> 0 us
  other arithmetic: 8.91 us -> 0 us
    all_gather x1 -> x0, blocking collectives: 11.5 us -> none  [local(): all_queries = lax.all_gather(queries, 'row', axis=0)]
    slice x3 -> x0, local copies, waits for them, and re-layouts: 6.7 us -> none  [the longest x1 2.93 us: local(): conv_one[:2].reshape(18, channels, channels)]
    convert_element_type x2 -> x0, other arithmetic: 3.63 us -> none  [the longest x1 1.86 us: local(): last = flipped[2].astype(f32)]
    pad x3 -> x1, local copies, waits for them, and re-layouts: 4.21 us -> 0.71 us  [local(): jnp.pad(tokens.reshape(height * width, channels), ((0, each - height * wi...]
    reduce_sum x3 -> x0, other arithmetic: 2.38 us -> none  [the longest x2 1.27 us: select_size(): return jnp.sum(jnp.where(marks, size_table, 0))]
    unnamed x35 -> x2, local copies, waits for them, and re-layouts: 5.17 us -> 2.94 us
    another operation x1 -> x0, other arithmetic: 1.78 us -> none  [local(): sizes = jnp.stack([row_count, col_count]).astype(jnp.int32)]
    pallas_call x3 -> x2, Pallas kernels: 86.1 us -> 85.3 us  [the longest x1 46.9 us: local(): remote_call(functools.partial(prior_kernel, counts), (shape((height * bre...]
  transfers between devices with their start and end apart: 1 -> 0, of which waited for: 0 -> 0; matrix products, arithmetic and copies ran while one was open for 15% -> 0% of each run, Pallas kernels for 25% -> 0%
where the time goes in v2:
time: 91.2 us; the launch traced here: 90.9 us
  Pallas kernels  85.3 us (94%)
  local copies, waits for them, and re-layouts  5.53 us (6%)
    pallas_call x1, Pallas kernels, local(): remote_call(functools.partial(prior_kernel, counts), (shape((height * bre...  46.9 us
    pallas_call x1, Pallas kernels, local(): remote_call(functools.partial(tail_kernel, counts, width), shape((2 * hei...  38.5 us
    unnamed x2, local copies, waits for them, and re-layouts  2.94 us

profile of v2, /device:TPU:0, one launch (start us, length us, event | category | flops | bytes accessed | tf_op | source)
XLA Modules:
  0.0 90.9 jit_solution(5913157205522663212)
XLA Ops:
  0.0 1.0 %reshape.12 = bf16[260,384]{1,0:T(8,128)(2,1)S(1)} reshape(bf16[13,20,384]{2,1,0:T(8,128)(2,1)} %param.14) | data formatting | bytes 399360 | tf_op jit(solution)/shard_map/reshape | solution.py:487
  1.0 0.7 pad.8.tokens
  1.7 1.1 %copy.15 = bf16[2,13,20,384]{3,2,1,0:T(8,128)(2,1)S(1)} copy(bf16[2,13,20,384]{3,0,2,1:T(2,128)(2,1)} %param.22) | data formatting | bytes 798720 | tf_op args[8]
  2.8 0.9 pad.9.cache_one
  3.7 46.9 %shard_map.136 = (f32[416,384]{1,0:T(8,128)}, f32[1248,192]{1,0:T(8,128)}, bf16[8,272,384]{2,1,0:T(8,128)(2,1)}, bf16[4,272,384]{2,1,0:T(8,128)(2,1)}, bf16[16,256,384]{2,1,0:T(8,128)(2,1)}) custom-call(s32[4]{0:T(128)} %row_sizes.3, s32[8]{0:T(128)} %col_sizes.3, bf16[272,384]{1,0:T(8,128)(2,1)} %pad.8.tokens, f32[384]{0:T(512)} %norm_gain.1, ...), custom_call_target="tpu_custom_call" | custom-call | flops 8999999488 | bytes 20000000 | tf_op jit(solution)/shard_map/pallas_call | solution.py:498
  50.6 38.5 %shard_map.137 = bf16[26,40,192]{2,1,0:T(8,128)(2,1)} custom-call(s32[4]{0:T(128)} %row_sizes.3, s32[8]{0:T(128)} %col_sizes.3, bf16[4,272,384]{2,1,0:T(8,128)(2,1)} %get-tuple-element.10.queries, bf16[8,272,384]{2,1,0:T(8,128)(2,1)} %get-tuple-element.11.keys, bf16[272,384]{1,0:T(8,128)(2,1)} %pad.8.tokens, bf16[384,384]{1,0:T(8,128)(2,1)} %value_weight.1, ...), custom_call_target="tpu_custom_call" | custom-call | flops 8999999488 | bytes 20000000 | tf_op jit(solution)/shard_map/pallas_call | solution.py:534
  89.0 1.9 %copy.17 = bf16[26,40,192]{2,1,0:T(8,128)(2,1)} copy(bf16[26,40,192]{2,1,0:T(8,128)(2,1)} %shard_map.137) | data formatting | bytes 798720

commit v3 on v2

--- a/solution.py
+++ b/solution.py
@@ -59,11 +59,14 @@
     return lax.broadcasted_iota(jnp.int32, shape, dim)
 
 
-def halo_copies(counts, sent, got, send_sems, recv_sems):
+def halo_copies(counts, lengths, sent, got, send_sems, recv_sems):
+    def piece(ref, k):
+        return ref.at[k, :, 0 : lengths[0 if k < 2 else (1 if k < 4 else 2)], :]
+
     return [
         pltpu.make_async_remote_copy(
-            src_ref=sent.at[k],
-            dst_ref=got.at[k],
+            src_ref=piece(sent, k),
+            dst_ref=piece(got, k),
             send_sem=send_sems.at[k],
             recv_sem=recv_sems.at[k],
             device_id=partner(counts, step),
@@ -93,7 +96,7 @@
     height, breadth, channels = frame.shape
     row, col = lax.axis_index("row"), lax.axis_index("col")
 
-    def piece(k):
+    def piece(k, count):
         ok = None
         step = steps[k]
         if step[0] != 0:
@@ -101,12 +104,12 @@
         if step[1] != 0:
             ok_col = (col > 0) if step[1] > 0 else (col < counts[1] - 1)
             ok = ok_col if ok is None else jnp.logical_and(ok, ok_col)
-        return got[k, f].astype(f32) * jnp.where(ok, 1.0, 0.0)
-
-    below, above = piece(0)[0:breadth], piece(1)[0:breadth]
-    right_side, left_side = piece(2), piece(3)
-    right_low, left_low = piece(4)[0:1], piece(5)[0:1]
-    right_top, left_top = piece(6)[0:1], piece(7)[0:1]
+        return got[k, f, 0 : round_up(count, 16), :].astype(f32) * jnp.where(ok, 1.0, 0.0)
+
+    below, above = piece(0, breadth), piece(1, breadth)
+    right_side, left_side = piece(2, height), piece(3, height)
+    right_low, left_low = piece(4, 1)[0:1], piece(5, 1)[0:1]
+    right_top, left_top = piece(6, 1)[0:1], piece(7, 1)[0:1]
     line_cols = iota3((breadth, channels), 0)
     below = jnp.where(line_cols == wide, right_low, below)
     above = jnp.where(line_cols == wide, right_top, above)
@@ -219,30 +222,32 @@
     return fast if cols % fast == 0 else 1
 
 
-def convolve_rows(shifted, frames, conv, product, start, size, breadth):
+def convolve_rows(shifted, frames, conv, product, start, size, breadth, first=0):
     part = None
     for f in range(frames):
         for a in range(3):
             for b in range(3):
                 rows = shifted[f, b, start + a * breadth : start + a * breadth + size, :]
-                term = product(rows, conv[f * 9 + a * 3 + b])
+                term = product(rows, conv[first + f * 9 + a * 3 + b])
                 part = term if part is None else part + term
     return part
 
 
-def prior_kernel(
-    counts, row_sizes, col_sizes, tokens, norm_gain, query_weight, key_weight,
-    cache_one, cache_two, conv_one, conv_two,
-    sum_one, sum_two, keys, queries, phase_weights,
-    sent_one, got_one, sent_two, got_two, shifted_one, shifted_two, held_one, held_two,
+def whole_kernel(
+    counts, width, row_sizes, col_sizes, tokens, norm_gain, query_weight, key_weight, value_weight,
+    out_weight, cache_one, gain_one, cache_two, gain_two, conv_one, conv_two, out,
+    sum_one, sum_two, keys, queries, phase_weights, parts, got_parts, bias, flat, small, fine_sum,
+    sent_one, got_one, sent_two, got_two, sent_new, got_new, sent_last, got_last,
+    shifted_one, shifted_two, shifted_new, shifted_last, held_one, held_two,
     send_sems, recv_sems, query_send, query_recv, fwd_sems, bwd_sems, fast_sems, key_recv, load_sems,
+    part_send, part_recv,
 ):
     row_count, col_count = counts
     row, col = lax.axis_index("row"), lax.axis_index("col")
     tall, wide = row_sizes[row], col_sizes[col]
     loads = [
         pltpu.make_async_copy(conv_two, held_two, load_sems.at[0]),
-        pltpu.make_async_copy(conv_one.at[0:18], held_one, load_sems.at[1]),
+        pltpu.make_async_copy(conv_one, held_one, load_sems.at[1]),
     ]
     for load in loads:
         load.start()
@@ -277,17 +282,20 @@
     for copy in query_copies:
         copy.start()
     breadth, fine_breadth = cache_one.shape[2], round_up(cache_two.shape[2] + 1, 16)
+    height = cache_one.shape[1]
+    lengths_one = (breadth, round_up(height, 16), 16)
+    lengths_two = (fine_breadth, round_up(2 * height, 16), 16)
     for f in range(2):
         last_line = cache_one[f, jnp.maximum(tall, 1) - 1].astype(f32)
         put_pieces(cache_one[f].astype(f32), last_line, f, tall, wide, sent_one)
-    halos_one = halo_copies(counts, sent_one, got_one, send_sems.at[0], recv_sems.at[0])
+    halos_one = halo_copies(counts, lengths_one, sent_one, got_one, send_sems.at[0], recv_sems.at[0])
     for copy in halos_one:
         copy.start()
     for f in range(2):
         last_line = widened(cache_two[f, 2 * jnp.maximum(tall, 1) - 1], fine_breadth)
         frame = widened(cache_two[f], fine_breadth)
         put_pieces(frame, last_line, f, 2 * tall, 2 * wide, sent_two)
-    halos_two = halo_copies(counts, sent_two, got_two, send_sems.at[1], recv_sems.at[1])
+    halos_two = halo_copies(counts, lengths_two, sent_two, got_two, send_sems.at[1], recv_sems.at[1])
     for copy in halos_two:
         copy.start()
     if slow > 1:
@@ -321,33 +329,21 @@
     for f in range(2):
         frame = widened(cache_two[f], fine_breadth)
         extend(frame, f, 2 * tall, 2 * wide, got_two, counts, shifted_two)
-    total = sum_two.shape[0]
-    size = total // 3 if total % 48 == 0 else total
-    for at in range(0, total, size):
-        sum_two[at : at + size, :] = convolve_rows(
-            shifted_two, 2, held_two, times_t, at, size, fine_breadth
-        )
+    fine_total = sum_two.shape[0]
+    fine_chunk = fine_total // 3 if fine_total % 48 == 0 else fine_total
+
+    def prior_two(part):
+        at = part * fine_chunk
+        if at < fine_total:
+            sum_two[at : at + fine_chunk, :] = convolve_rows(
+                shifted_two, 2, held_two, times_t, at, fine_chunk, fine_breadth
+            )
+
+    prior_two(0)
     finish()
     for copy in query_copies:
         copy.wait()
-
-
-def tail_kernel(
-    counts, width, row_sizes, col_sizes, queries, keys, tokens, value_weight, out_weight,
-    gain_one, gain_two, sum_one, sum_two, conv_two, conv_one, out,
-    parts, bias, held_one, got_parts, sent_one, got_one, sent_two, got_two,
-    shifted_one, shifted_two, flat, small, fine_sum,
-    part_send, part_recv, send_sems, recv_sems, load_sem,
-):
-    row_count, col_count = counts
-    row, col = lax.axis_index("row"), lax.axis_index("col")
-    tall, wide = row_sizes[row], col_sizes[col]
-    load = pltpu.make_async_copy(conv_one.at[18:27], held_one, load_sem)
-    load.start()
-    others = [(wrapped(row, d, row_count), col) for d in range(1, row_count)]
-    greet(others + [partner(counts, step) for step in steps if step[1] != 0])
     each, channels = tokens.shape
-    height, breadth, _ = small.shape
     slot = lax.broadcasted_iota(jnp.int32, (1, each), 1)
     slot_row = jnp.zeros((1, each), jnp.int32)
     for r in range(1, height + 1):
@@ -390,6 +386,7 @@
         )
         copies[-1].start()
     partial_of(row)
+    prior_two(1)
     for copy in copies:
         copy.wait()
     blocks = [parts[row]] + [got_parts[d] for d in range(row_count - 1)]
@@ -412,35 +409,35 @@
     for r in range(height):
         small[r, 0:width, :] = flat[r * width : (r + 1) * width, :]
     frame = small[...]
-    put_pieces(frame, small[jnp.maximum(tall, 1) - 1], 0, tall, wide, sent_one)
-    halos = halo_copies(counts, sent_one, got_one, send_sems.at[0], recv_sems.at[0])
+    put_pieces(frame, small[jnp.maximum(tall, 1) - 1], 0, tall, wide, sent_new)
+    halos = halo_copies(counts, lengths_one, sent_new, got_new, send_sems.at[2], recv_sems.at[2])
     for copy in halos:
         copy.start()
-    load.wait()
+    prior_two(2)
     for copy in halos:
         copy.wait()
-    extend(frame, 0, tall, wide, got_one, counts, shifted_one)
-    size = height * breadth
-    y_one = sum_one[...] + convolve_rows(shifted_one, 1, held_one, times, 0, size, breadth)
+    extend(frame, 0, tall, wide, got_new, counts, shifted_new)
+    size_one = height * breadth
+    y_one = sum_one[...] + convolve_rows(shifted_new, 1, held_one, times, 0, size_one, breadth, 18)
     y_one = y_one.astype(bf16).astype(f32)
     small[...] = silu(rms_scale(y_one, gain_two[...][None, :])).reshape(height, breadth, channels)
     frame = small[...]
-    put_pieces(frame, small[jnp.maximum(tall, 1) - 1], 0, tall, wide, sent_two)
-    halos = halo_copies(counts, sent_two, got_two, send_sems.at[1], recv_sems.at[1])
+    put_pieces(frame, small[jnp.maximum(tall, 1) - 1], 0, tall, wide, sent_last)
+    halos = halo_copies(counts, lengths_one, sent_last, got_last, send_sems.at[3], recv_sems.at[3])
     for copy in halos:
         copy.start()
     for copy in halos:
         copy.wait()
-    extend(frame, 0, tall, wide, got_two, counts, shifted_two)
+    extend(frame, 0, tall, wide, got_last, counts, shifted_last)
     for p in range(2):
         for q in range(2):
-            phase = jnp.zeros((size, conv_two.shape[1]), f32)
+            phase = jnp.zeros((size_one, phase_weights.shape[1]), f32)
             for a in range(2):
                 for b in range(2):
                     first = (p + a) * breadth
                     phase += times_t(
-                        shifted_two[0, q + b, first : first + size, :],
-                        conv_two[p * 8 + q * 4 + a * 2 + b],
+                        shifted_last[0, q + b, first : first + size_one, :],
+                        phase_weights[p * 8 + q * 4 + a * 2 + b],
                     )
             for i in range(height):
                 for lane in range(fine_sum.shape[0]):
@@ -448,14 +445,13 @@
                         i * breadth : (i + 1) * breadth, lane * 128 : (lane + 1) * 128
                     ]
     fine_height, fine_narrow, channels_out = out.shape
-    fine_breadth = sum_two.shape[1]
     fine_cols = lax.broadcasted_iota(jnp.int32, (fine_narrow, channels_out), 0)
     for i in range(fine_height):
         keep = jnp.logical_and(fine_cols < 2 * wide, i < 2 * tall)
         for lane in range(fine_sum.shape[0]):
             place = slice(lane * 128, min(lane * 128 + 128, channels_out))
             count = place.stop - place.start
-            line = fine_sum[lane, i, 0:fine_narrow, 0:count] + sum_two[i, 0:fine_narrow, place]
+            line = fine_sum[lane, i, 0:fine_narrow, 0:count] + sum_two[i * fine_breadth : i * fine_breadth + fine_narrow, place]
             out[i, :, place] = jnp.where(keep[:, place], line, 0.0).astype(bf16)
 
 
@@ -495,27 +491,38 @@
     slow = cols // fast
     vm, sm, dma = pltpu.VMEM, pltpu.SMEM, pltpu.SemaphoreType.DMA
     shape = jax.ShapeDtypeStruct
-    sum_one, sum_two, keys, queries, phase_weights = remote_call(
-        functools.partial(prior_kernel, counts),
-        (
-            shape((height * breadth, channels), f32),
-            shape((2 * height * fine_breadth, channels_out), f32),
-            shape((cols, each, channels), bf16),
-            shape((rows, each, channels), bf16),
-            shape((16, lanes_out, channels), bf16),
-        ),
-        [sm] * 2 + [vm] * 6 + [pl.ANY] * 2,
+    return remote_call(
+        functools.partial(whole_kernel, counts, width),
+        shape((2 * height, 2 * width, channels_out), bf16),
+        [sm] * 2 + [vm] * 10 + [pl.ANY] * 2,
         [
+            vm((height * breadth, channels), f32),
+            vm((2 * height * fine_breadth, channels_out), f32),
+            vm((cols, each, channels), bf16),
+            vm((rows, each, channels), bf16),
+            vm((16, lanes_out, channels), bf16),
+            vm((rows, each, channels + 128), bf16),
+            vm((rows - 1, each, channels + 128), bf16),
+            vm((round_up(cols, 8), each), f32),
+            vm((each, channels), f32),
+            vm((height, breadth, channels), f32),
+            vm((lanes_out // 128, 2 * height, 2 * breadth, 128), f32),
             vm((8, 2, line_one, channels), bf16),
             vm((8, 2, line_one, channels), bf16),
             vm((8, 2, line_two, channels), bf16),
             vm((8, 2, line_two, channels), bf16),
+            vm((8, 1, line_one, channels), bf16),
+            vm((8, 1, line_one, channels), bf16),
+            vm((8, 1, line_one, channels), bf16),
+            vm((8, 1, line_one, channels), bf16),
             vm((2, 3, (height + 2) * breadth, channels), bf16),
             vm((2, 3, (2 * height + 2) * fine_breadth, channels), bf16),
-            vm((18, channels, channels), bf16),
+            vm((1, 3, (height + 2) * breadth, channels), bf16),
+            vm((1, 3, (height + 2) * breadth, channels), bf16),
+            vm((27, channels, channels), bf16),
             vm((27, channels_out, channels), bf16),
-            dma((2, 8)),
-            dma((2, 8)),
+            dma((4, 8)),
+            dma((4, 8)),
             dma((rows - 1,)),
             dma((rows - 1,)),
             dma((slow,)),
@@ -523,43 +530,14 @@
             dma((max(fast - 1, 1), slow)),
             dma((cols,)),
             dma((2,)),
+            dma((rows - 1,)),
+            dma((rows - 1,)),
         ],
         1,
-        9_000_000_000,
+        18_000_000_000,
     )(
-        row_sizes, col_sizes, flat, norm_gain, query_weight, key_weight,
-        wide_one, cache_two, kernels_one, kernels_two,
-    )
-    sum_two = sum_two.reshape(2 * height, fine_breadth, channels_out)
-    return remote_call(
-        functools.partial(tail_kernel, counts, width),
-        shape((2 * height, 2 * width, channels_out), bf16),
-        [sm] * 2 + [vm] * 10 + [pl.ANY],
-        [
-            vm((rows, each, channels + 128), bf16),
-            vm((round_up(cols, 8), each), f32),
-            vm((9, channels, channels), bf16),
-            vm((rows - 1, each, channels + 128), bf16),
-            vm((8, 1, line_one, channels), bf16),
-            vm((8, 1, line_one, channels), bf16),
-            vm((8, 1, line_one, channels), bf16),
-            vm((8, 1, line_one, channels), bf16),
-            vm((1, 3, (height + 2) * breadth, channels), bf16),
-            vm((1, 3, (height + 2) * breadth, channels), bf16),
-            vm((each, channels), f32),
-            vm((height, breadth, channels), f32),
-            vm((lanes_out // 128, 2 * height, 2 * breadth, 128), f32),
-            dma((rows - 1,)),
-            dma((rows - 1,)),
-            dma((2, 8)),
-            dma((2, 8)),
-            dma,
-        ],
-        2,
-        9_000_000_000,
-    )(
-        row_sizes, col_sizes, queries, keys, flat, value_weight, out_weight,
-        gain_one, gain_two, sum_one, sum_two, phase_weights, kernels_one,
+        row_sizes, col_sizes, flat, norm_gain, query_weight, key_weight, value_weight, out_weight,
+        wide_one, gain_one, cache_two, gain_two, kernels_one, kernels_two,
     )
 
 

time: 91.2 us -> 75 us (0.82)
  Pallas kernels: 85.3 us -> 69.3 us
    pallas_call x2 -> x1, Pallas kernels: 85.3 us -> 69.3 us  [local(): remote_call(functools.partial(whole_kernel, counts, width), shape((2 * he...]
where the time goes in v3:
time: 75 us; the launch traced here: 74.8 us
  Pallas kernels  69.3 us (92%)
  local copies, waits for them, and re-layouts  5.51 us (7%)
    pallas_call x1, Pallas kernels, local(): remote_call(functools.partial(whole_kernel, counts, width), shape((2 * he...  69.3 us
    unnamed x2, local copies, waits for them, and re-layouts  2.94 us

profile of v3, /device:TPU:0, one launch (start us, length us, event | category | flops | bytes accessed | tf_op | source)
XLA Modules:
  0.0 74.8 jit_solution(826372976399273541)
XLA Ops:
  0.0 1.0 %reshape.9 = bf16[260,384]{1,0:T(8,128)(2,1)S(1)} reshape(bf16[13,20,384]{2,1,0:T(8,128)(2,1)} %param.14) | data formatting | bytes 399360 | tf_op jit(solution)/shard_map/reshape | solution.py:483
  1.0 0.7 pad.8.tokens
  1.7 1.1 %copy.15 = bf16[2,13,20,384]{3,2,1,0:T(8,128)(2,1)S(1)} copy(bf16[2,13,20,384]{3,0,2,1:T(2,128)(2,1)} %param.22) | data formatting | bytes 798720 | tf_op args[8]
  2.8 0.9 %pad.9.cache_one = bf16[2,13,32,384]{3,2,1,0:T(8,128)(2,1)} pad(bf16[2,13,20,384]{3,2,1,0:T(8,128)(2,1)S(1)} %copy.15, bf16[]{:T(256)} %constant.2.clone.1), padding=0_0x0_0x0_12x0_0 | pad | bytes 1038338 | tf_op jit(solution)/shard_map/jit(_pad)/pad | solution.py:484
  3.6 69.3 %shard_map.136 = bf16[26,40,192]{2,1,0:T(8,128)(2,1)} custom-call(s32[4]{0:T(128)} %row_sizes.1, s32[8]{0:T(128)} %col_sizes.1, bf16[272,384]{1,0:T(8,128)(2,1)} %pad.8.tokens, f32[384]{0:T(512)} %norm_gain.1, bf16[384,384]{1,0:T(8,128)(2,1)} %query_weight.1, bf16[384,384]{1,0:T(8,128)(2,1)} %key_weight.1, bf16[384,384]{1,0:T(8,128)(2,1)} %value_weight.1, ...), custom_call_target="tpu_custom_call" | custom-call | flops 17999998976 | bytes 20000000 | tf_op jit(solution)/shard_map/pallas_call | solution.py:494
  72.9 1.9 %copy.17 = bf16[26,40,192]{2,1,0:T(8,128)(2,1)} copy(bf16[26,40,192]{2,1,0:T(8,128)(2,1)} %shard_map.136) | data formatting | bytes 798720

commit v4 on v3

--- a/solution.py
+++ b/solution.py
@@ -52,7 +52,7 @@
     barrier = pltpu.get_barrier_semaphore()
     for device in devices:
         pl.semaphore_signal(barrier, inc=1, device_id=device, device_id_type=MESH)
-    pl.semaphore_wait(barrier, len(devices))
+    return lambda: pl.semaphore_wait(barrier, len(devices))
 
 
 def iota3(shape, dim):
@@ -234,9 +234,9 @@
 
 
 def whole_kernel(
-    counts, width, row_sizes, col_sizes, tokens, norm_gain, query_weight, key_weight, value_weight,
+    counts, row_sizes, col_sizes, tokens, norm_gain, query_weight, key_weight, value_weight,
     out_weight, cache_one, gain_one, cache_two, gain_two, conv_one, conv_two, out,
-    sum_one, sum_two, keys, queries, phase_weights, parts, got_parts, bias, flat, small, fine_sum,
+    sum_one, sum_two, keys, queries, phase_weights, parts, got_parts, bias, flat, small, wide_one, fine_sum,
     sent_one, got_one, sent_two, got_two, sent_new, got_new, sent_last, got_last,
     shifted_one, shifted_two, shifted_new, shifted_last, held_one, held_two,
     send_sems, recv_sems, query_send, query_recv, fwd_sems, bwd_sems, fast_sems, key_recv, load_sems,
@@ -258,16 +258,23 @@
         (row, wrapped(col, step * fast, col_count)) for step in ((1, -1) if slow > 1 else ())
     ]
     others = [(wrapped(row, d, row_count), col) for d in range(1, row_count)]
-    greet(
+    greeted = greet(
         others + fast_others + line
         + [partner(counts, step) for step in steps if step[1] != 0]
     )
-    normed = rms_scale(tokens[...].astype(f32), norm_gain[...][None, :]).astype(bf16)
+    height, width, channels = tokens.shape
+    each = flat.shape[0]
+    for r in range(height):
+        flat[r * width : (r + 1) * width, :] = tokens[r].astype(f32)
+    if each > height * width:
+        flat[height * width :, :] = jnp.zeros((each - height * width, channels), f32)
+    normed = rms_scale(flat[...], norm_gain[...][None, :]).astype(bf16)
     keys[col] = normed
+    query = times(normed, query_weight[...]).astype(bf16)
+    unit = math.log2(math.e) / math.sqrt(channels)
+    queries[row] = (times_t(query, key_weight[...]) * unit).astype(bf16)
+    greeted()
     start()
-    query = times(normed, query_weight[...]).astype(bf16)
-    unit = math.log2(math.e) / math.sqrt(tokens.shape[1])
-    queries[row] = (times_t(query, key_weight[...]) * unit).astype(bf16)
     query_copies = [
         pltpu.make_async_remote_copy(
             src_ref=queries.at[row],
@@ -281,13 +288,16 @@
     ]
     for copy in query_copies:
         copy.start()
-    breadth, fine_breadth = cache_one.shape[2], round_up(cache_two.shape[2] + 1, 16)
-    height = cache_one.shape[1]
+    breadth, fine_breadth = small.shape[1], round_up(cache_two.shape[2] + 1, 16)
     lengths_one = (breadth, round_up(height, 16), 16)
     lengths_two = (fine_breadth, round_up(2 * height, 16), 16)
+    wide_one[...] = jnp.zeros_like(wide_one)
     for f in range(2):
-        last_line = cache_one[f, jnp.maximum(tall, 1) - 1].astype(f32)
-        put_pieces(cache_one[f].astype(f32), last_line, f, tall, wide, sent_one)
+        for r in range(height):
+            wide_one[f, r, 0:width, :] = cache_one[f, r].astype(f32)
+    for f in range(2):
+        last_line = wide_one[f, jnp.maximum(tall, 1) - 1]
+        put_pieces(wide_one[f], last_line, f, tall, wide, sent_one)
     halos_one = halo_copies(counts, lengths_one, sent_one, got_one, send_sems.at[0], recv_sems.at[0])
     for copy in halos_one:
         copy.start()
@@ -301,21 +311,10 @@
     if slow > 1:
         hop(1)
     loads[0].wait()
-    channels_out = held_two.shape[1]
-    phase_weights[:, channels_out:, :] = jnp.zeros_like(phase_weights[:, channels_out:, :])
-    for p in range(2):
-        for q in range(2):
-            for a in range(2):
-                for b in range(2):
-                    rows_in = ((0,), (1, 2))[a] if p == 0 else ((0, 1), (2,))[a]
-                    cols_in = ((0,), (1, 2))[b] if q == 0 else ((0, 1), (2,))[b]
-                    taps = [held_two[18 + 3 * i + j].astype(f32) for i in rows_in for j in cols_in]
-                    total = functools.reduce(jnp.add, taps).astype(bf16)
-                    phase_weights[p * 8 + q * 4 + a * 2 + b, 0:channels_out, :] = total
     for copy in halos_one:
         copy.wait()
     for f in range(2):
-        extend(cache_one[f].astype(f32), f, tall, wide, got_one, counts, shifted_one)
+        extend(wide_one[f], f, tall, wide, got_one, counts, shifted_one)
     if slow > 2:
         hop(2)
     loads[1].wait()
@@ -340,10 +339,6 @@
             )
 
     prior_two(0)
-    finish()
-    for copy in query_copies:
-        copy.wait()
-    each, channels = tokens.shape
     slot = lax.broadcasted_iota(jnp.int32, (1, each), 1)
     slot_row = jnp.zeros((1, each), jnp.int32)
     for r in range(1, height + 1):
@@ -354,6 +349,9 @@
         bias[c : c + 1, :] = jnp.where(usable, 0.0, masked_score)
     masks = jnp.concatenate([bias[c : c + 1, :] for c in range(col_count)], axis=1)
     lanes = lax.broadcasted_iota(jnp.int32, (each, 128), 1)
+    finish()
+    for copy in query_copies:
+        copy.wait()
 
     def partial_of(target):
         all_keys = keys[...].reshape(col_count * each, channels)
@@ -403,7 +401,7 @@
     mean = (mean / total).astype(bf16)
     attention = times(mean, value_weight[...]).astype(bf16)
     projected = times(attention, out_weight[...])
-    mixed = (tokens[...].astype(f32) + projected).astype(bf16).astype(f32)
+    mixed = (flat[...] + projected).astype(bf16).astype(f32)
     flat[...] = silu(rms_scale(mixed, gain_one[...][None, :]))
     small[...] = jnp.zeros_like(small)
     for r in range(height):
@@ -426,6 +424,17 @@
     halos = halo_copies(counts, lengths_one, sent_last, got_last, send_sems.at[3], recv_sems.at[3])
     for copy in halos:
         copy.start()
+    channels_out = held_two.shape[1]
+    phase_weights[:, channels_out:, :] = jnp.zeros_like(phase_weights[:, channels_out:, :])
+    for p in range(2):
+        for q in range(2):
+            for a in range(2):
+                for b in range(2):
+                    rows_in = ((0,), (1, 2))[a] if p == 0 else ((0, 1), (2,))[a]
+                    cols_in = ((0,), (1, 2))[b] if q == 0 else ((0, 1), (2,))[b]
+                    taps = [held_two[18 + 3 * i + j].astype(f32) for i in rows_in for j in cols_in]
+                    total = functools.reduce(jnp.add, taps).astype(bf16)
+                    phase_weights[p * 8 + q * 4 + a * 2 + b, 0:channels_out, :] = total
     for copy in halos:
         copy.wait()
     extend(frame, 0, tall, wide, got_last, counts, shifted_last)
@@ -480,8 +489,6 @@
     fine_breadth = round_up(2 * width + 1, 16)
     each = round_up(height * width, 16)
 
-    flat = jnp.pad(tokens.reshape(height * width, channels), ((0, each - height * width), (0, 0)))
-    wide_one = jnp.pad(cache_one, ((0, 0), (0, 0), (0, breadth - width), (0, 0)))
     kernels_one = conv_one.reshape(27, channels, channels)
     kernels_two = jnp.swapaxes(conv_two, 3, 4).reshape(27, channels_out, channels)
     line_one = max(breadth, round_up(height, 16))
@@ -492,7 +499,7 @@
     vm, sm, dma = pltpu.VMEM, pltpu.SMEM, pltpu.SemaphoreType.DMA
     shape = jax.ShapeDtypeStruct
     return remote_call(
-        functools.partial(whole_kernel, counts, width),
+        functools.partial(whole_kernel, counts),
         shape((2 * height, 2 * width, channels_out), bf16),
         [sm] * 2 + [vm] * 10 + [pl.ANY] * 2,
         [
@@ -506,6 +513,7 @@
             vm((round_up(cols, 8), each), f32),
             vm((each, channels), f32),
             vm((height, breadth, channels), f32),
+            vm((2, height, breadth, channels), f32),
             vm((lanes_out // 128, 2 * height, 2 * breadth, 128), f32),
             vm((8, 2, line_one, channels), bf16),
             vm((8, 2, line_one, channels), bf16),
@@ -536,8 +544,8 @@
         1,
         18_000_000_000,
     )(
-        row_sizes, col_sizes, flat, norm_gain, query_weight, key_weight, value_weight, out_weight,
-        wide_one, gain_one, cache_two, gain_two, kernels_one, kernels_two,
+        row_sizes, col_sizes, tokens, norm_gain, query_weight, key_weight, value_weight, out_weight,
+        cache_one, gain_one, cache_two, gain_two, kernels_one, kernels_two,
     )
 
 

time: 75 us -> 72.9 us (0.972)
  local copies, waits for them, and re-layouts: 5.51 us -> 3.71 us
    pad x2 -> x0, local copies, waits for them, and re-layouts: 1.59 us -> none  [the longest x1 0.88 us: local(): jnp.pad(cache_one, ((0, 0), (0, 0), (0, breadth - width), (0, 0)))]
    reshape x1 -> x0, local copies, waits for them, and re-layouts: 0.98 us -> none  [local(): tokens.reshape(height * width, channels)]
    unnamed x2, local copies, waits for them, and re-layouts: 2.94 us -> 3.71 us
where the time goes in v4:
time: 72.9 us; the launch traced here: 72.7 us
  Pallas kernels  69 us (95%)
  local copies, waits for them, and re-layouts  3.71 us (5%)
    pallas_call x1, Pallas kernels, local(): remote_call(functools.partial(whole_kernel, counts), shape((2 * height, 2...  69 us
    unnamed x2, local copies, waits for them, and re-layouts  3.71 us

profile of v4, /device:TPU:0, one launch (start us, length us, event | category | flops | bytes accessed | tf_op | source)
XLA Modules:
  0.0 72.7 jit_solution(2649195801784246880)
XLA Ops:
  0.0 1.8 %copy.15.cache_one = bf16[2,13,20,384]{3,2,1,0:T(8,128)(2,1)} copy(bf16[2,13,20,384]{3,0,2,1:T(2,128)(2,1)} %param.22) | data formatting | bytes 798720 | tf_op args[8]
  1.8 69.0 %shard_map.136 = bf16[26,40,192]{2,1,0:T(8,128)(2,1)} custom-call(s32[4]{0:T(128)} %row_sizes.1, s32[8]{0:T(128)} %col_sizes.1, bf16[13,20,384]{2,1,0:T(8,128)(2,1)} %tokens.1, f32[384]{0:T(512)} %norm_gain.1, bf16[384,384]{1,0:T(8,128)(2,1)} %query_weight.1, bf16[384,384]{1,0:T(8,128)(2,1)} %key_weight.1, bf16[384,384]{1,0:T(8,128)(2,1)} %value_weight.1, ...), custom_call_target="tpu_custom_call" | custom-call | flops 17999998976 | bytes 20000000 | tf_op jit(solution)/shard_map/pallas_call | solution.py:501
  70.9 1.9 %copy.17 = bf16[26,40,192]{2,1,0:T(8,128)(2,1)} copy(bf16[26,40,192]{2,1,0:T(8,128)(2,1)} %shard_map.136) | data formatting | bytes 798720
